TPU v7x, 32 devices: a whole 2x2x4 slice. The times are simulated.
32 devices in a mesh: ctx: 16 (over z, y, core), tp: 2 (over x).
Axes of the slice: x: 2, y: 2, z: 4, core: 2. Of those that a mesh axis runs over, the one named last changes fastest.
Arguments:
- query_in: bfloat16 [256, 4096], P('tp', 'ctx'), may hold values from -6 to 6
- key_in: bfloat16 [256, 4096], P('tp', 'ctx'), may hold values from -6 to 6
- value_in: bfloat16 [256, 4096], P('tp', 'ctx'), may hold values from -6 to 6
- short_kernel: float32 [3, 256, 7], P(None, 'tp'), may hold values from -2 to 2
- basis_weight: float32 [64, 33], replicated, may hold values from -96 to 96
- basis_bias: float32 [64], replicated, may hold values from -3.140625 to 3.140625
- filter_proj: float32 [256, 64], P('tp'), may hold values from -0.75 to 0.75
- decay_rate: float32 [256], P('tp'), as said below
- skip_gain: float32 [256], P('tp'), may hold values from -3 to 3
- grad_out: bfloat16 [256, 4096], P('tp', 'ctx'), may hold values from -6 to 6
Outputs:
- mixed: bfloat16 [256, 4096], P('tp', 'ctx')
- grad_query: bfloat16 [256, 4096], P('tp', 'ctx')
- grad_key: bfloat16 [256, 4096], P('tp', 'ctx')
- grad_value: bfloat16 [256, 4096], P('tp', 'ctx')
- grad_proj: float32 [256, 64], P('tp')
- grad_basis: float32 [64, 33], replicated
Inputs may be any that keep to these rules, and one draw needn't show every extreme that they name: decay_rate is positive in every channel.
All inputs are finite; a program needn't handle non-finite values.
Results may differ from a plain program's by a relative error of at most 0.0066.
Values may be sent and summed in bfloat16 or wider, within the bound.
A program may use at most 64 MiB of HBM per device.

v0:
```python
import math

import jax
import jax.numpy as jnp
from jax import lax
from jax.sharding import PartitionSpec as P

PRECISE = lax.Precision.HIGHEST


def passed_along(value, axis, steps):
    count = lax.axis_size(axis)
    leading, last = (max(0, -steps), min(count, count - steps))
    return lax.ppermute(value, axis, [(source, source + steps) for source in range(leading, last)])


def features(offset_pos, num_pos, seq_total, num_freq):
    positions = offset_pos + jnp.arange(num_pos, dtype=jnp.int32)
    pieces = [positions.astype(jnp.float32) / seq_total]
    for harmonic in range(1, num_freq + 1):
        angles = (harmonic * positions % seq_total).astype(jnp.float32) * (
            2.0 * math.pi / seq_total
        )
        pieces.append(jnp.cos(angles))
        pieces.append(jnp.sin(angles))
    return jnp.stack(pieces)


def window(decay_rate, offset_pos, num_pos, seq_total):
    positions = (offset_pos + jnp.arange(num_pos, dtype=jnp.int32)).astype(jnp.float32)
    energy = jnp.expm1(-2.0 * decay_rate) / jnp.expm1(-2.0 * decay_rate / seq_total)
    return (
        jnp.exp(-(decay_rate[:, None] * positions[None, :]) / seq_total) / jnp.sqrt(energy)[:, None]
    )


def featurize_rim(signal, before, kernel):
    extended = jnp.concatenate([before, signal], axis=1).astype(jnp.float32)
    num_taps = kernel.shape[1]
    rim_len = num_taps - 1
    num_tok = signal.shape[1]
    result = kernel[:, 0:1] * extended[:, rim_len:]
    for offset in range(1, num_taps):
        result = (
            result
            + kernel[:, offset : offset + 1]
            * extended[:, rim_len - offset : rim_len - offset + num_tok]
        )
    return result


def featurize_back(signal, following, kernel):
    extended = jnp.concatenate([signal, following], axis=1).astype(jnp.float32)
    num_taps = kernel.shape[1]
    num_tok = signal.shape[1]
    result = kernel[:, 0:1] * extended[:, :num_tok]
    for offset in range(1, num_taps):
        result = result + kernel[:, offset : offset + 1] * extended[:, offset : offset + num_tok]
    return result


def tables(num_rows, num_cols, modulus):
    row_ids = jnp.arange(num_rows, dtype=jnp.int32)[:, None]
    col_ids = jnp.arange(num_cols, dtype=jnp.int32)[None, :]
    angles = (row_ids * col_ids % modulus).astype(jnp.float32) * (-2.0 * math.pi / modulus)
    return (jnp.cos(angles), jnp.sin(angles))


def spectrum(signal, outer, twiddle, inner):
    num_chan = signal.shape[0]
    folded = signal.reshape(num_chan, outer[0].shape[1], inner[0].shape[0])
    section_re = jnp.einsum("kt,nts->nks", outer[0], folded, precision=PRECISE)
    section_im = jnp.einsum("kt,nts->nks", outer[1], folded, precision=PRECISE)
    turned_re = section_re * twiddle[0] - section_im * twiddle[1]
    turned_im = section_re * twiddle[1] + section_im * twiddle[0]
    spec_re = jnp.einsum("nks,sj->nkj", turned_re, inner[0], precision=PRECISE) - jnp.einsum(
        "nks,sj->nkj", turned_im, inner[1], precision=PRECISE
    )
    spec_im = jnp.einsum("nks,sj->nkj", turned_re, inner[1], precision=PRECISE) + jnp.einsum(
        "nks,sj->nkj", turned_im, inner[0], precision=PRECISE
    )
    return (spec_re, spec_im)


def restore(spec_re, spec_im, outer, twiddle, inner):
    num_chan = spec_re.shape[0]
    padded_len = outer[0].shape[0] * inner[0].shape[0]
    back_re = jnp.einsum("nkj,sj->nks", spec_re, inner[0], precision=PRECISE) + jnp.einsum(
        "nkj,sj->nks", spec_im, inner[1], precision=PRECISE
    )
    back_im = jnp.einsum("nkj,sj->nks", spec_im, inner[0], precision=PRECISE) - jnp.einsum(
        "nkj,sj->nks", spec_re, inner[1], precision=PRECISE
    )
    turned_re = back_re * twiddle[0] + back_im * twiddle[1]
    turned_im = back_im * twiddle[0] - back_re * twiddle[1]
    result = jnp.einsum("kt,nks->nts", outer[0], turned_re, precision=PRECISE) + jnp.einsum(
        "kt,nks->nts", outer[1], turned_im, precision=PRECISE
    )
    return result.reshape(num_chan, -1) * (1.0 / padded_len)


def convolve_forward(carried_chan, filter_chan, own_skip, transform_tables):
    outer, twiddle, inner = transform_tables
    carried_wide = carried_chan.astype(jnp.float32)
    carried_re, carried_im = spectrum(carried_wide, outer, twiddle, inner)
    filter_re, filter_im = spectrum(filter_chan.astype(jnp.float32), outer, twiddle, inner)
    conv_chan = restore(
        filter_re * carried_re - filter_im * carried_im,
        filter_re * carried_im + filter_im * carried_re,
        outer,
        twiddle,
        inner,
    )
    long_chan = (conv_chan + own_skip[:, None] * carried_wide).astype(jnp.bfloat16)
    return (long_chan, (carried_re, carried_im, filter_re, filter_im))


def convolve_backward(grad_chan, spectra, own_skip, transform_tables):
    outer, twiddle, inner = transform_tables
    carried_re, carried_im, filter_re, filter_im = spectra
    grad_chan_wide = grad_chan.astype(jnp.float32)
    grad_re, grad_im = spectrum(grad_chan_wide, outer, twiddle, inner)
    carried_grad_chan = (
        restore(
            filter_re * grad_re + filter_im * grad_im,
            filter_re * grad_im - filter_im * grad_re,
            outer,
            twiddle,
            inner,
        )
        + own_skip[:, None] * grad_chan_wide
    ).astype(jnp.bfloat16)
    filter_grad_chan = restore(
        carried_re * grad_re + carried_im * grad_im,
        carried_re * grad_im - carried_im * grad_re,
        outer,
        twiddle,
        inner,
    ).astype(jnp.bfloat16)
    return (carried_grad_chan, filter_grad_chan)


def on_device(
    query_in,
    key_in,
    value_in,
    short_kernel,
    basis_weight,
    basis_bias,
    filter_proj,
    decay_rate,
    skip_gain,
    grad_out,
):
    ctx_size = lax.axis_size("ctx")
    ctx_rank = lax.axis_index("ctx")
    tp_size = lax.axis_size("tp")
    num_tok = query_in.shape[1]
    chan_local = query_in.shape[0]
    seq_total = num_tok * ctx_size
    all_channels = chan_local * tp_size
    num_freq = (basis_weight.shape[1] - 1) // 2
    feat_width = basis_weight.shape[0]
    rim_len = short_kernel.shape[2] - 1
    tok_start = ctx_rank * num_tok
    rim_edge = num_tok - rim_len
    per_dev = chan_local // ctx_size
    chan_start = ctx_rank * per_dev
    own_skip = lax.dynamic_slice_in_dim(skip_gain, chan_start, per_dev)
    proj_scale = 1.0 / math.sqrt(seq_total)
    basis_scale = math.sqrt(feat_width / (seq_total * all_channels))
    before = passed_along(
        (query_in[:, rim_edge:], key_in[:, rim_edge:], value_in[:, rim_edge:]), "ctx", 1
    )
    query_feat = featurize_rim(query_in, before[0], short_kernel[0])
    key_feat = featurize_rim(key_in, before[1], short_kernel[1])
    value_feat = featurize_rim(value_in, before[2], short_kernel[2])
    carried = (key_feat * value_feat).astype(jnp.bfloat16)
    grad_wide = grad_out.astype(jnp.float32)
    grad_long = (grad_wide * query_feat).astype(jnp.bfloat16)
    basis_rows = features(tok_start, num_tok, seq_total, num_freq)
    hidden_in = (
        jnp.dot(basis_weight, basis_rows, precision=PRECISE, preferred_element_type=jnp.float32)
        + basis_bias[:, None]
    )
    activation = jnp.sin(hidden_in)
    envelope = window(decay_rate, tok_start, num_tok, seq_total)
    filter_tok = (
        jnp.dot(filter_proj, activation, precision=PRECISE, preferred_element_type=jnp.float32)
        * envelope
    ).astype(jnp.bfloat16)
    inner_len = 2 * ctx_size
    transform_tables = (
        tables(num_tok, num_tok // 2, num_tok),
        tables(num_tok, inner_len, 2 * seq_total),
        tables(inner_len, inner_len, inner_len),
    )
    spread = (
        lax.all_to_all(carried, "ctx", split_axis=0, concat_axis=1, tiled=True),
        lax.all_to_all(filter_tok, "ctx", split_axis=0, concat_axis=1, tiled=True),
    )
    carried_chan = spread[0]
    filter_chan = spread[1]
    long_chan, spectra = convolve_forward(carried_chan, filter_chan, own_skip, transform_tables)
    long_tok = lax.all_to_all(long_chan, "ctx", split_axis=1, concat_axis=0, tiled=True)
    grad_chan = lax.all_to_all(grad_long, "ctx", split_axis=0, concat_axis=1, tiled=True)
    carried_grad_chan, filter_grad_chan = convolve_backward(
        grad_chan, spectra, own_skip, transform_tables
    )
    returned = (
        lax.all_to_all(carried_grad_chan, "ctx", split_axis=1, concat_axis=0, tiled=True),
        lax.all_to_all(filter_grad_chan, "ctx", split_axis=1, concat_axis=0, tiled=True),
    )
    carried_grad = returned[0]
    filter_grad_tok = returned[1]
    long_wide = long_tok.astype(jnp.float32)
    mixed = (query_feat * long_wide).astype(jnp.bfloat16)
    grad_query_feat = (grad_wide * long_wide).astype(jnp.bfloat16)
    grad_raw = filter_grad_tok.astype(jnp.float32) * envelope
    part_proj = jnp.dot(
        grad_raw, activation.T, precision=PRECISE, preferred_element_type=jnp.float32
    )
    grad_hidden = jnp.dot(
        filter_proj.T, grad_raw, precision=PRECISE, preferred_element_type=jnp.float32
    ) * jnp.cos(hidden_in)
    part_basis = jnp.dot(
        grad_hidden, basis_rows.T, precision=PRECISE, preferred_element_type=jnp.float32
    )
    grad_proj = lax.psum(part_proj, "ctx") * proj_scale
    grad_basis = lax.psum(part_basis, ("ctx", "tp")) * basis_scale
    carried_grad_wide = carried_grad.astype(jnp.float32)
    grad_key_feat = (carried_grad_wide * value_feat).astype(jnp.bfloat16)
    grad_value_feat = (carried_grad_wide * key_feat).astype(jnp.bfloat16)
    following = passed_along(
        (grad_query_feat[:, :rim_len], grad_key_feat[:, :rim_len], grad_value_feat[:, :rim_len]),
        "ctx",
        -1,
    )
    grad_query = featurize_back(grad_query_feat, following[0], short_kernel[0]).astype(jnp.bfloat16)
    grad_key = featurize_back(grad_key_feat, following[1], short_kernel[1]).astype(jnp.bfloat16)
    grad_value = featurize_back(grad_value_feat, following[2], short_kernel[2]).astype(jnp.bfloat16)
    return (mixed, grad_query, grad_key, grad_value, grad_proj, grad_basis)


def solution(mesh):
    return jax.shard_map(
        on_device,
        mesh=mesh,
        in_specs=(
            P("tp", "ctx"),
            P("tp", "ctx"),
            P("tp", "ctx"),
            P(None, "tp", None),
            P(),
            P(),
            P("tp", None),
            P("tp"),
            P("tp"),
            P("tp", "ctx"),
        ),
        out_specs=(
            P("tp", "ctx"),
            P("tp", "ctx"),
            P("tp", "ctx"),
            P("tp", "ctx"),
            P("tp", None),
            P(),
        ),
        check_vma=False,
    )
```

profile of v0, /device:TPU:0, one launch (start us, length us, event | category | flops | bytes accessed | tf_op | source)
XLA Modules:
  0.0 200.1 jit_solution(8017786709411005207)
XLA Ops:
  0.6 0.8 slice.242
  1.5 2.3 %collective-permute-start = (bf16[128,6]{1,0:T(8,128)(2,1)S(1)}, bf16[128,6]{1,0:T(8,128)(2,1)S(1)}, u32[]{:S(2)}, u32[]{:S(2)}) collective-permute-start(bf16[128,6]{1,0:T(8,128)(2,1)S(1)} %slice.242), channel_id=1, source_target_pairs={{0,2},{2,4},{4,6},{6,8},{8,10},{10,12},{12,14},{14,16},{16,18},{18... | collective-permute-start | bytes 4616 | tf_op jit(solution)/shard_map/ppermute | solution.py:14
  5.3 0.6 copy-done.9
  7.2 1.0 fusion.8
  8.1 7.3 %all-to-all-start = ((bf16[16,8,256]{2,1,0:T(8,128)(2,1)}), bf16[16,8,256]{2,1,0:T(8,128)(2,1)S(1)}, u32[]{:S(2)}, u32[]{:S(2)}) async-start(bf16[16,8,256]{2,1,0:T(8,128)(2,1)} %fusion.8), calls=%async_computation | async-start | bytes 131072 | tf_op jit(solution)/shard_map/all_to_all | solution.py:200
  15.6 2.4 %collective-permute-start.2 = (bf16[128,6]{1,0:T(8,128)(2,1)S(1)}, bf16[128,6]{1,0:T(8,128)(2,1)S(1)}, u32[]{:S(2)}, u32[]{:S(2)}) collective-permute-start(bf16[128,6]{1,0:T(8,128)(2,1)S(1)} %slice.274), channel_id=1, source_target_pairs={{0,2},{2,4},{4,6},{6,8},{8,10},{10,12},{12,14},{14,16},{16,18},{18... | collective-permute-start | bytes 4616 | tf_op jit(solution)/shard_map/ppermute | solution.py:14
  18.1 3.7 %collective-permute-start.1 = (bf16[128,6]{1,0:T(8,128)(2,1)S(1)}, bf16[128,6]{1,0:T(8,128)(2,1)S(1)}, u32[]{:S(2)}, u32[]{:S(2)}) collective-permute-start(bf16[128,6]{1,0:T(8,128)(2,1)S(1)} %slice.258), channel_id=1, source_target_pairs={{0,2},{2,4},{4,6},{6,8},{8,10},{10,12},{12,14},{14,16},{16,18},{18... | collective-permute-start | bytes 4616 | tf_op jit(solution)/shard_map/ppermute | solution.py:14
  22.0 0.6 copy-done.8
  22.9 0.7 copy-done.1
  23.6 1.0 fusion.109
  24.6 4.7 %all-to-all-start.3 = ((bf16[16,8,256]{2,1,0:T(8,128)(2,1)}), bf16[16,8,256]{2,1,0:T(8,128)(2,1)S(1)}, u32[]{:S(2)}, u32[]{:S(2)}) async-start(bf16[16,8,256]{2,1,0:T(8,128)(2,1)} %get-tuple-element.10), calls=%async_computation.3 | async-start | bytes 131072 | tf_op jit(solution)/shard_map/all_to_all | solution.py:206
  29.5 0.8 convolution_bitcast_fusion.4
  30.3 0.8 convolution_bitcast_fusion.5
  32.7 3.5 %all-to-all-done.3 = bf16[16,8,256]{2,1,0:T(8,128)(2,1)S(1)} async-done(((bf16[16,8,256]{2,1,0:T(8,128)(2,1)}), bf16[16,8,256]{2,1,0:T(8,128)(2,1)S(1)}, u32[]{:S(2)}, u32[]{:S(2)}) %all-to-all-start.3) | async-done | bytes 65568 | tf_op jit(solution)/shard_map/all_to_all | solution.py:206
  36.4 0.8 convolution_bitcast_fusion
  37.2 0.8 convolution_bitcast_fusion.1
  42.4 0.9 fusion.20
  43.3 0.9 fusion.2
  44.6 0.7 fusion.90
  45.3 3.5 %all-to-all-start.4 = ((bf16[8,16,256]{2,0,1:T(8,128)(2,1)}), bf16[8,16,256]{2,0,1:T(8,128)(2,1)S(1)}, u32[]{:S(2)}, u32[]{:S(2)}) async-start(bf16[8,16,256]{2,0,1:T(8,128)(2,1)} %fusion.90), calls=%async_computation.4 | async-start | bytes 131072 | tf_op jit(solution)/shard_map/all_to_all | solution.py:211
  49.0 6.6 %all-to-all-done.4 = bf16[8,16,256]{2,0,1:T(8,128)(2,1)S(1)} async-done(((bf16[8,16,256]{2,0,1:T(8,128)(2,1)}), bf16[8,16,256]{2,0,1:T(8,128)(2,1)S(1)}, u32[]{:S(2)}, u32[]{:S(2)}) %all-to-all-start.4) | async-done | bytes 65568 | tf_op jit(solution)/shard_map/all_to_all | solution.py:211
  56.1 1.3 collective-permute-start.5
  57.8 0.6 fusion.108
  58.4 3.7 %all-to-all-start.1 = ((bf16[16,8,256]{2,1,0:T(8,128)(2,1)}), bf16[16,8,256]{2,1,0:T(8,128)(2,1)S(1)}, u32[]{:S(2)}, u32[]{:S(2)}) async-start(bf16[16,8,256]{2,1,0:T(8,128)(2,1)} %fusion.108), calls=%async_computation.1 | async-start | bytes 131072 | tf_op jit(solution)/shard_map/all_to_all | solution.py:199
  62.1 1.5 collective-permute-start.4
  63.7 1.0 fusion.37
  64.7 0.9 collective-permute-done.4
  65.6 1.0 fusion.44
  66.6 2.4 %all-to-all-done.1 = bf16[16,8,256]{2,1,0:T(8,128)(2,1)S(1)} async-done(((bf16[16,8,256]{2,1,0:T(8,128)(2,1)}), bf16[16,8,256]{2,1,0:T(8,128)(2,1)S(1)}, u32[]{:S(2)}, u32[]{:S(2)}) %all-to-all-start.1) | async-done | bytes 65568 | tf_op jit(solution)/shard_map/all_to_all | solution.py:199
  69.2 0.8 convolution_bitcast_fusion.2
  70.0 0.8 convolution_bitcast_fusion.3
  72.3 0.7 multiply_add_fusion
  74.8 0.9 fusion.13
  75.7 0.9 fusion.9
  76.9 0.7 copy.104
  77.6 5.2 %all-to-all-start.5 = ((bf16[8,16,256]{2,0,1:T(8,128)(2,1)}), bf16[8,16,256]{2,0,1:T(8,128)(2,1)S(1)}, u32[]{:S(2)}, u32[]{:S(2)}) async-start(bf16[8,16,256]{2,0,1:T(8,128)(2,1)} %copy.104), calls=%async_computation.5 | async-start | bytes 131072 | tf_op jit(solution)/shard_map/all_to_all | solution.py:212
  84.6 0.9 fusion.27
  85.5 0.9 fusion.4
  86.7 0.7 fusion.91
  87.5 2.2 %all-to-all-done.5 = bf16[8,16,256]{2,0,1:T(8,128)(2,1)S(1)} async-done(((bf16[8,16,256]{2,0,1:T(8,128)(2,1)}), bf16[8,16,256]{2,0,1:T(8,128)(2,1)S(1)}, u32[]{:S(2)}, u32[]{:S(2)}) %all-to-all-start.5) | async-done | bytes 65568 | tf_op jit(solution)/shard_map/all_to_all | solution.py:212
  89.7 3.8 %all-to-all-start.2 = ((bf16[8,16,256]{2,0,1:T(8,128)(2,1)}), bf16[8,16,256]{2,0,1:T(8,128)(2,1)S(1)}, u32[]{:S(2)}, u32[]{:S(2)}) async-start(bf16[8,16,256]{2,0,1:T(8,128)(2,1)} %fusion.91), calls=%async_computation.2 | async-start | bytes 131072 | tf_op jit(solution)/shard_map/all_to_all | solution.py:205
  94.1 40.9 %psum.15 = f32[64,33]{0,1:T(8,128)S(1)} all-reduce(f32[64,33]{0,1:T(8,128)S(1)} %fusion.431), channel_id=1, replica_groups=mesh['ctx'=16,'tp'=2] {'ctx','tp'}, use_global_device_ids=true, to_apply=%region_1.2 | all-reduce | flops 2112 | bytes 16896 | tf_op jit(solution)/shard_map/psum | solution.py:230
  135.4 59.3 %psum.14 = f32[128,64]{0,1:T(8,128)S(1)} all-reduce(f32[128,64]{0,1:T(8,128)S(1)} %fusion.107), channel_id=1, replica_groups=mesh['ctx'=16,'tp'=2] {'ctx'}, use_global_device_ids=true, to_apply=%region_0.1 | all-reduce | flops 8192 | bytes 65536 | tf_op jit(solution)/shard_map/psum | solution.py:229
  194.7 0.6 broadcast_multiply_fusion
  195.3 0.7 fusion.31
  196.0 1.3 collective-permute-start.3
  197.9 1.2 collective-permute-done.3
  199.1 1.0 fusion.51
  (102 shorter events, 18.3 us)
Async XLA Ops:
  0.6 6.5 %copy-start = (f32[128,64]{0,1:T(8,128)S(1)}, f32[128,64]{0,1:T(8,128)}, u32[]{:S(2)}) copy-start(f32[128,64]{0,1:T(8,128)} %param.16) | copy-start | bytes 98308
  1.5 21.3 %collective-permute-start = (bf16[128,6]{1,0:T(8,128)(2,1)S(1)}, bf16[128,6]{1,0:T(8,128)(2,1)S(1)}, u32[]{:S(2)}, u32[]{:S(2)}) collective-permute-start(bf16[128,6]{1,0:T(8,128)(2,1)S(1)} %slice.242), channel_id=1, source_target_pairs={{0,2},{2,4},{4,6},{6,8},{8,10},{10,12},{12,14},{14,16},{16,18},{18... | collective-permute-start | bytes 4616 | tf_op jit(solution)/shard_map/ppermute | solution.py:14
  5.3 0.7 copy-start.9
  6.0 0.7 copy-start.5
  6.0 0.7 copy-start.7
  8.1 7.4 %copy-start.3 = (bf16[128,256]{1,0:T(8,128)(2,1)S(1)}, bf16[128,256]{1,0:T(8,128)(2,1)}, u32[]{:S(2)}) copy-start(bf16[128,256]{1,0:T(8,128)(2,1)} %param.12) | copy-start | bytes 196612
  8.1 16.5 %all-to-all-start = ((bf16[16,8,256]{2,1,0:T(8,128)(2,1)}), bf16[16,8,256]{2,1,0:T(8,128)(2,1)S(1)}, u32[]{:S(2)}, u32[]{:S(2)}) async-start(bf16[16,8,256]{2,1,0:T(8,128)(2,1)} %fusion.8), calls=%async_computation | async-start | bytes 131072 | tf_op jit(solution)/shard_map/all_to_all | solution.py:200
  15.5 2.5 %copy-start.4 = (bf16[128,256]{1,0:T(8,128)(2,1)S(1)}, bf16[128,256]{1,0:T(8,128)(2,1)}, u32[]{:S(2)}) copy-start(bf16[128,256]{1,0:T(8,128)(2,1)} %param.11) | copy-start | bytes 196612
  15.6 6.2 %copy-start.6 = (f32[3,128,7]{1,2,0:T(8,128)S(1)}, f32[3,128,7]{1,2,0:T(8,128)}, u32[]{:S(2)}) copy-start(f32[3,128,7]{1,2,0:T(8,128)} %param.13) | copy-start | bytes 32260
  15.6 33.2 %collective-permute-start.2 = (bf16[128,6]{1,0:T(8,128)(2,1)S(1)}, bf16[128,6]{1,0:T(8,128)(2,1)S(1)}, u32[]{:S(2)}, u32[]{:S(2)}) collective-permute-start(bf16[128,6]{1,0:T(8,128)(2,1)S(1)} %slice.274), channel_id=1, source_target_pairs={{0,2},{2,4},{4,6},{6,8},{8,10},{10,12},{12,14},{14,16},{16,18},{18... | collective-permute-start | bytes 4616 | tf_op jit(solution)/shard_map/ppermute | solution.py:14
  18.1 4.6 %copy-start.2 = (bf16[128,256]{1,0:T(8,128)(2,1)S(1)}, bf16[128,256]{1,0:T(8,128)(2,1)}, u32[]{:S(2)}) copy-start(bf16[128,256]{1,0:T(8,128)(2,1)} %param.10) | copy-start | bytes 196612
  18.1 30.8 %collective-permute-start.1 = (bf16[128,6]{1,0:T(8,128)(2,1)S(1)}, bf16[128,6]{1,0:T(8,128)(2,1)S(1)}, u32[]{:S(2)}, u32[]{:S(2)}) collective-permute-start(bf16[128,6]{1,0:T(8,128)(2,1)S(1)} %slice.258), channel_id=1, source_target_pairs={{0,2},{2,4},{4,6},{6,8},{8,10},{10,12},{12,14},{14,16},{16,18},{18... | collective-permute-start | bytes 4616 | tf_op jit(solution)/shard_map/ppermute | solution.py:14
  22.0 0.7 copy-start.8
  22.8 0.8 copy-start.1
  24.6 11.6 %all-to-all-start.3 = ((bf16[16,8,256]{2,1,0:T(8,128)(2,1)}), bf16[16,8,256]{2,1,0:T(8,128)(2,1)S(1)}, u32[]{:S(2)}, u32[]{:S(2)}) async-start(bf16[16,8,256]{2,1,0:T(8,128)(2,1)} %get-tuple-element.10), calls=%async_computation.3 | async-start | bytes 131072 | tf_op jit(solution)/shard_map/all_to_all | solution.py:206
  45.3 10.4 %all-to-all-start.4 = ((bf16[8,16,256]{2,0,1:T(8,128)(2,1)}), bf16[8,16,256]{2,0,1:T(8,128)(2,1)S(1)}, u32[]{:S(2)}, u32[]{:S(2)}) async-start(bf16[8,16,256]{2,0,1:T(8,128)(2,1)} %fusion.90), calls=%async_computation.4 | async-start | bytes 131072 | tf_op jit(solution)/shard_map/all_to_all | solution.py:211
  56.1 7.6 %collective-permute-start.5 = (bf16[128,6]{1,0:T(8,128)(2,1)S(1)}, bf16[128,6]{1,0:T(8,128)(2,1)S(1)}, u32[]{:S(2)}, u32[]{:S(2)}) collective-permute-start(bf16[128,6]{1,0:T(8,128)(2,1)S(1)} %slice.349), channel_id=1, source_target_pairs={{2,0},{4,2},{6,4},{8,6},{10,8},{12,10},{14,12},{16,14},{18,16},{20... | collective-permute-start | bytes 4616 | tf_op jit(solution)/shard_map/ppermute | solution.py:14
  58.4 10.6 %all-to-all-start.1 = ((bf16[16,8,256]{2,1,0:T(8,128)(2,1)}), bf16[16,8,256]{2,1,0:T(8,128)(2,1)S(1)}, u32[]{:S(2)}, u32[]{:S(2)}) async-start(bf16[16,8,256]{2,1,0:T(8,128)(2,1)} %fusion.108), calls=%async_computation.1 | async-start | bytes 131072 | tf_op jit(solution)/shard_map/all_to_all | solution.py:199
  62.1 3.4 %collective-permute-start.4 = (bf16[128,6]{1,0:T(8,128)(2,1)S(1)}, bf16[128,6]{1,0:T(8,128)(2,1)S(1)}, u32[]{:S(2)}, u32[]{:S(2)}) collective-permute-start(bf16[128,6]{1,0:T(8,128)(2,1)S(1)} %slice.341), channel_id=1, source_target_pairs={{2,0},{4,2},{6,4},{8,6},{10,8},{12,10},{14,12},{16,14},{18,16},{20... | collective-permute-start | bytes 4616 | tf_op jit(solution)/shard_map/ppermute | solution.py:14
  77.6 12.1 %all-to-all-start.5 = ((bf16[8,16,256]{2,0,1:T(8,128)(2,1)}), bf16[8,16,256]{2,0,1:T(8,128)(2,1)S(1)}, u32[]{:S(2)}, u32[]{:S(2)}) async-start(bf16[8,16,256]{2,0,1:T(8,128)(2,1)} %copy.104), calls=%async_computation.5 | async-start | bytes 131072 | tf_op jit(solution)/shard_map/all_to_all | solution.py:212
  89.7 105.6 %all-to-all-start.2 = ((bf16[8,16,256]{2,0,1:T(8,128)(2,1)}), bf16[8,16,256]{2,0,1:T(8,128)(2,1)S(1)}, u32[]{:S(2)}, u32[]{:S(2)}) async-start(bf16[8,16,256]{2,0,1:T(8,128)(2,1)} %fusion.91), calls=%async_computation.2 | async-start | bytes 131072 | tf_op jit(solution)/shard_map/all_to_all | solution.py:205
  196.0 3.1 %collective-permute-start.3 = (bf16[128,6]{1,0:T(8,128)(2,1)S(1)}, bf16[128,6]{1,0:T(8,128)(2,1)S(1)}, u32[]{:S(2)}, u32[]{:S(2)}) collective-permute-start(bf16[128,6]{1,0:T(8,128)(2,1)S(1)} %slice.333), channel_id=1, source_target_pairs={{2,0},{4,2},{6,4},{8,6},{10,8},{12,10},{14,12},{16,14},{18,16},{20... | collective-permute-start | bytes 4616 | tf_op jit(solution)/shard_map/ppermute | solution.py:14
where the time goes:
time: 201 us; the launch traced here: 200 us
  blocking collectives  100 us (50%)
  starting transfers between devices  40.7 us (20%)
  matrix products  24.1 us (12%)
  waiting for transfers between devices  16.8 us (8%)
  other arithmetic  10.7 us (5%)
  local copies, waits for them, and re-layouts  6.19 us (3%)
    psum x1, blocking collectives, on_device(): grad_proj = lax.psum(part_proj, 'ctx') * proj_scale  59.3 us
    psum x1, blocking collectives, on_device(): grad_basis = lax.psum(part_basis, ('ctx', 'tp')) * basis_scale  40.9 us
    ppermute x6, starting transfers between devices, passed_along(): lax.ppermute(value, axis, [(source, source + steps) for source in range(l...  12.5 us
    all_to_all x1, starting transfers between devices, on_device(): lax.all_to_all(filter_tok, 'ctx', split_axis=0, concat_axis=1, tiled=True)  7.35 us
    all_to_all x1, waiting for transfers between devices, on_device(): lax.all_to_all(carried_grad_chan, 'ctx', split_axis=1, concat_axis=0, til...  6.63 us
    all_to_all x1, starting transfers between devices, on_device(): lax.all_to_all(filter_grad_chan, 'ctx', split_axis=1, concat_axis=0, tile...  5.16 us
    all_to_all x1, starting transfers between devices, on_device(): lax.all_to_all(grad_long, 'ctx', split_axis=0, concat_axis=1, tiled=True)  4.66 us
  transfers between devices with their start and end apart: 12, of which 6 were waited for; matrix products, arithmetic and copies ran while one was open for 13% of the time, Pallas kernels for 0%

commit v1 on v0

v1 whole, which is shorter than its diff:
```python
import functools
import math

import jax
import jax.numpy as jnp
import ml_dtypes
import numpy as np
from jax import lax
from jax.experimental import pallas as pl
from jax.experimental.pallas import tpu as pltpu
from jax.sharding import PartitionSpec as P

MESH = pl.DeviceIdType.MESH
BF16 = jnp.bfloat16
F32 = jnp.float32
LANES = 128
BAND = 40


def halves(table):
    high = table.astype(ml_dtypes.bfloat16)
    low = (table - high.astype(np.float64)).astype(ml_dtypes.bfloat16)
    return high, low


def constant_tables(seq_total, chans, num_freq):
    blocks = seq_total // LANES
    kept = blocks + 1
    period = 2 * blocks
    spec_rows = -(-kept * chans // 8) * 8
    eye = np.eye(chans)
    k1 = np.arange(kept)
    n1 = np.arange(blocks)
    n2 = np.arange(LANES)
    turn = 2.0 * np.pi * ((k1[:, None] * n1[None, :]) % period) / period
    fwd = np.zeros((2, spec_rows, blocks * chans))
    fwd[0, : kept * chans] = np.kron(np.cos(turn), eye)
    fwd[1, : kept * chans] = np.kron(-np.sin(turn), eye)
    weight = np.where((k1 == 0) | (k1 == blocks), 1.0, 2.0)[:, None] / (2.0 * seq_total)
    back = np.zeros((2, spec_rows, blocks * chans))
    back[0, : kept * chans] = np.kron(weight * np.cos(turn), eye)
    back[1, : kept * chans] = np.kron(-weight * np.sin(turn), eye)
    back = back.reshape(2 * spec_rows, blocks * chans).T.copy()
    fwd = fwd.reshape(2 * spec_rows, blocks * chans)
    twist = 2.0 * np.pi * ((k1[:, None] * n2[None, :]) % (2 * seq_total)) / (2 * seq_total)
    twiddle = np.zeros((2, spec_rows, LANES))
    twiddle[0, : kept * chans] = np.repeat(np.cos(twist), chans, axis=0)
    twiddle[1, : kept * chans] = np.repeat(-np.sin(twist), chans, axis=0)
    small = 2.0 * np.pi * ((n2[:, None] * n2[None, :]) % LANES) / LANES
    cos, sin = np.cos(small), np.sin(small)
    inner = np.block([[cos, -sin], [sin, cos]])
    inner_back = np.block([[cos, sin], [-sin, cos]])
    positions = np.arange(seq_total)
    basis = np.zeros((BAND, seq_total))
    basis[0] = positions / seq_total
    for harmonic in range(1, num_freq + 1):
        angles = 2.0 * np.pi * ((harmonic * positions) % seq_total) / seq_total
        basis[2 * harmonic - 1] = np.cos(angles)
        basis[2 * harmonic] = np.sin(angles)
    basis[2 * num_freq + 1] = 1.0
    first = basis.astype(ml_dtypes.bfloat16)
    rest = basis - first.astype(np.float64)
    second = rest.astype(ml_dtypes.bfloat16)
    third = (rest - second.astype(np.float64)).astype(ml_dtypes.bfloat16)
    rim = np.zeros((16, seq_total), ml_dtypes.bfloat16)
    basis_table = np.concatenate([first, second, third, first, second, first, rim])
    return (
        basis_table,
        *halves(fwd),
        *halves(back),
        *halves(inner),
        *halves(inner_back),
        twiddle.astype(np.float32),
    )


def dot(left, right):
    return jnp.dot(left, right, preferred_element_type=F32)


def dot_lanes(left, right):
    return lax.dot_general(left, right, (((1,), (1,)), ((), ())), preferred_element_type=F32)


def split(value):
    high = value.astype(BF16)
    return high, (value - high.astype(F32)).astype(BF16)


def sine_cosine(angle):
    quarter = jnp.floor(angle * (2.0 / math.pi) + 0.5)
    rest = angle - quarter * 1.5703125
    rest = rest - quarter * 4.837512969970703125e-4
    rest = rest - quarter * 7.54978995489188216e-8
    square = rest * rest
    sine = rest + rest * square * (
        -1.6666654611e-1 + square * (8.3321608736e-3 + square * -1.9515295891e-4)
    )
    cosine = (
        1.0
        - 0.5 * square
        + square
        * square
        * (4.166664568298827e-2 + square * (-1.388731625493765e-3 + square * 2.443315711809948e-5))
    )
    turns = quarter.astype(jnp.int32)
    odd = (turns & 1) == 1
    sin_out = jnp.where(odd, cosine, sine)
    cos_out = jnp.where(odd, sine, cosine)
    sin_out = jnp.where((turns & 2) == 2, -sin_out, sin_out)
    cos_out = jnp.where(((turns + 1) & 2) == 2, -cos_out, cos_out)
    return sin_out, cos_out


def mixer_kernel(
    dims,
    kv_ref,
    qg_ref,
    params_ref,
    weight_ref,
    basis_ref,
    fwd_hi,
    fwd_lo,
    back_hi,
    back_lo,
    inner_hi,
    inner_lo,
    inv_hi,
    inv_lo,
    twiddle_ref,
    mq_out,
    kv_out,
    proj_out,
    basis_out,
    kv_in,
    qg_in,
    mq_send,
    kv_send,
    mq_back,
    kv_back,
    act_buf,
    cos_buf,
    filt_buf,
    rows_buf,
    part_buf,
    part_in,
    sum_buf,
    sum_in,
    gp_buf,
    gp_in,
    send_sems,
    recv_sems,
):
    ctx_size, tp_size, chans, seq_total, taps, feat, emb, tp_chans = dims
    me = lax.axis_index("ctx")
    my_tp = lax.axis_index("tp")
    blocks = seq_total // LANES
    rows = blocks * chans
    spec_rows = twiddle_ref.shape[1]
    slab = 2 * chans
    all_size = ctx_size * tp_size
    my_id = my_tp * ctx_size + me
    chunk = 512

    def others(body):
        def step(offset, carry):
            body(lax.rem(me + offset, ctx_size))
            return carry

        lax.fori_loop(1, ctx_size, step, 0)

    def all_others(body):
        def step(offset, carry):
            other = lax.rem(my_id + offset, all_size)
            body(lax.rem(other, ctx_size), other // ctx_size)
            return carry

        lax.fori_loop(1, all_size, step, 0)

    barrier = pltpu.get_barrier_semaphore()

    def greet(ctx, tp):
        pl.semaphore_signal(
            barrier, inc=1, device_id={"ctx": ctx, "tp": tp}, device_id_type=MESH
        )

    all_others(greet)
    pl.semaphore_wait(barrier, all_size - 1)

    def push(src, dst, lane, ctx, tp):
        pltpu.make_async_remote_copy(
            src_ref=src,
            dst_ref=dst,
            send_sem=send_sems.at[lane],
            recv_sem=recv_sems.at[lane],
            device_id={"ctx": ctx, "tp": tp},
            device_id_type=MESH,
        ).start()

    def settle(ref, sem, count):
        part = ref.at[pl.ds(0, count)]
        pltpu.make_async_copy(part, part, sem).wait()

    others(lambda peer: push(kv_ref.at[peer], kv_in.at[me], 0, peer, my_tp))
    others(lambda peer: push(qg_ref.at[peer], qg_in.at[me], 1, peer, my_tp))
    kv_in[me] = kv_ref[me]
    qg_in[me] = qg_ref[me]

    params = params_ref[me]

    def column(index):
        wide = jnp.broadcast_to(params[:, index : index + 1], (8, LANES))
        return jnp.concatenate([wide] * (rows // 8), axis=0)

    tap_at = feat
    decay = column(feat + 3 * taps)
    inv_energy = column(feat + 3 * taps + 1)
    skip = column(feat + 3 * taps + 2)

    lane_ids = lax.broadcasted_iota(jnp.int32, (rows, LANES), 1)
    row_ids = lax.broadcasted_iota(jnp.int32, (rows, LANES), 0)
    positions = ((row_ids // chans) * LANES + lane_ids).astype(F32)
    envelope = jnp.exp(-(decay * positions) / seq_total) * inv_energy

    weight = weight_ref[...]
    w_one = weight.astype(BF16)
    w_rest = weight - w_one.astype(F32)
    w_two = w_rest.astype(BF16)
    w_three = (w_rest - w_two.astype(F32)).astype(BF16)
    place = lax.broadcasted_iota(jnp.int32, weight.shape, 1)
    w_stack = jnp.where(
        place < 3 * BAND,
        w_one.astype(F32),
        jnp.where(place < 5 * BAND, w_two.astype(F32), w_three.astype(F32)),
    ).astype(BF16)

    own_proj = params[:, :feat]
    proj_hi, proj_lo = split(own_proj)
    proj_hi = proj_hi.astype(F32)
    proj_lo = proj_lo.astype(F32)
    proj_stack = jnp.concatenate(
        [
            jnp.concatenate([proj_hi, proj_hi], axis=1),
            jnp.concatenate([proj_lo, proj_lo], axis=1),
        ],
        axis=0,
    ).astype(BF16)

    def filter_step(index, carry):
        start = pl.multiple_of(index * chunk, chunk)
        here = pl.ds(start, chunk)
        hidden = dot(w_stack, basis_ref[:, here])
        act, cosine = sine_cosine(hidden)
        cos_buf[:, here] = cosine
        act_hi, act_lo = split(act)
        act_buf[0:feat, here] = act_hi
        act_buf[feat : 2 * feat, here] = act_lo
        both = dot(proj_stack, act_buf[:, here])
        piece = both[0:8] + both[8:16]
        for block in range(chunk // LANES):
            at = pl.multiple_of((index * (chunk // LANES) + block) * chans, chans)
            filt_buf[pl.ds(at, chans), :] = piece[
                0:chans, block * LANES : (block + 1) * LANES
            ]
        return carry

    lax.fori_loop(0, seq_total // chunk, filter_step, 0)
    filt = (filt_buf[...] * envelope).astype(BF16)

    def spectrum(signal):
        outer = dot(fwd_hi[...], signal) + dot(fwd_lo[...], signal)
        out_re, out_im = outer[:spec_rows], outer[spec_rows:]
        tw_re, tw_im = twiddle_ref[0], twiddle_ref[1]
        turned = jnp.concatenate(
            [out_re * tw_re - out_im * tw_im, out_re * tw_im + out_im * tw_re], axis=1
        )
        high, low = split(turned)
        spec = dot(high, inner_hi[...]) + dot(high, inner_lo[...]) + dot(low, inner_hi[...])
        return spec[:, :LANES], spec[:, LANES:]

    def restore(spec_re, spec_im):
        high, low = split(jnp.concatenate([spec_re, spec_im], axis=1))
        section = dot(high, inv_hi[...]) + dot(high, inv_lo[...]) + dot(low, inv_hi[...])
        sec_re, sec_im = section[:, :LANES], section[:, LANES:]
        tw_re, tw_im = twiddle_ref[0], twiddle_ref[1]
        turned = jnp.concatenate(
            [sec_re * tw_re + sec_im * tw_im, sec_im * tw_re - sec_re * tw_im], axis=0
        )
        high, low = split(turned)
        return dot(back_hi[...], high) + dot(back_lo[...], high) + dot(back_hi[...], low)

    def to_rows(ref, index):
        if slab % 16 == 0:
            return ref[:, index].reshape(rows, LANES).astype(F32)
        for source in range(ctx_size):
            rows_buf[source * slab : (source + 1) * slab, :] = ref[source, index].astype(F32)
        return rows_buf[...]

    def from_rows(ref, index, value):
        if slab % 16 == 0:
            ref[:, index] = value.reshape(ctx_size, slab, LANES)
        else:
            rows_buf[...] = value.astype(F32)
            for target in range(ctx_size):
                ref[target, index] = rows_buf[target * slab : (target + 1) * slab, :].astype(BF16)

    blank = jnp.zeros((chans, LANES), F32)

    def down(value):
        if chans % 8 == 0:
            return jnp.concatenate([blank, value[: rows - chans]], axis=0)
        return jnp.where(row_ids < chans, 0.0, pltpu.roll(value, chans, 0))

    def up(value):
        if chans % 8 == 0:
            return jnp.concatenate([value[chans:], blank], axis=0)
        return jnp.where(row_ids >= rows - chans, 0.0, pltpu.roll(value, rows - chans, 0))

    def featurize(signal, which):
        result = column(tap_at + which * taps) * signal
        for offset in range(1, taps):
            turned = pltpu.roll(signal, offset, 1)
            shifted = jnp.where(lane_ids < offset, down(turned), turned)
            result = result + column(tap_at + which * taps + offset) * shifted
        return result

    def featurize_back(signal, which):
        result = column(tap_at + which * taps) * signal
        for offset in range(1, taps):
            turned = pltpu.roll(signal, LANES - offset, 1)
            shifted = jnp.where(lane_ids >= LANES - offset, up(turned), turned)
            result = result + column(tap_at + which * taps + offset) * shifted
        return result

    filt_re, filt_im = spectrum(filt)

    settle(kv_in, recv_sems.at[0], ctx_size - 1)
    key_feat = featurize(to_rows(kv_in, 0), 1)
    value_feat = featurize(to_rows(kv_in, 1), 2)
    carried = (key_feat * value_feat).astype(BF16)
    carried_re, carried_im = spectrum(carried)

    long_out = restore(
        filt_re * carried_re - filt_im * carried_im, filt_re * carried_im + filt_im * carried_re
    )
    long_out = (long_out + skip * carried.astype(F32)).astype(BF16).astype(F32)

    settle(qg_in, recv_sems.at[1], ctx_size - 1)
    query_feat = featurize(to_rows(qg_in, 0), 0)
    grad_wide = to_rows(qg_in, 1)
    from_rows(mq_send, 0, (query_feat * long_out).astype(BF16))
    grad_query_feat = (grad_wide * long_out).astype(BF16).astype(F32)
    from_rows(mq_send, 1, featurize_back(grad_query_feat, 0).astype(BF16))
    others(lambda peer: push(mq_send.at[peer], mq_back.at[me], 2, peer, my_tp))

    grad_long = (grad_wide * query_feat).astype(BF16)
    grad_re, grad_im = spectrum(grad_long)

    carried_grad = restore(
        filt_re * grad_re + filt_im * grad_im, filt_re * grad_im - filt_im * grad_re
    )
    carried_grad = (carried_grad + skip * grad_long.astype(F32)).astype(BF16).astype(F32)
    grad_key_feat = (carried_grad * value_feat).astype(BF16).astype(F32)
    grad_value_feat = (carried_grad * key_feat).astype(BF16).astype(F32)
    from_rows(kv_send, 0, featurize_back(grad_key_feat, 1).astype(BF16))
    from_rows(kv_send, 1, featurize_back(grad_value_feat, 2).astype(BF16))
    others(lambda peer: push(kv_send.at[peer], kv_back.at[me], 3, peer, my_tp))

    filter_grad = restore(
        carried_re * grad_re + carried_im * grad_im, carried_re * grad_im - carried_im * grad_re
    )
    grad_raw = filter_grad.astype(BF16).astype(F32) * envelope
    if chans % 8 == 0:
        raw_wide = jnp.concatenate(
            [grad_raw[block * chans : (block + 1) * chans] for block in range(blocks)], axis=1
        )
    else:
        rows_buf[...] = grad_raw
        raw_wide = jnp.concatenate(
            [
                jnp.concatenate(
                    [
                        rows_buf[block * chans : (block + 1) * chans, :],
                        jnp.zeros((8 - chans, LANES), F32),
                    ],
                    axis=0,
                )
                for block in range(blocks)
            ],
            axis=1,
        )
    raw_hi, raw_lo = split(raw_wide)
    raw_hi = raw_hi.astype(F32)
    raw_lo = raw_lo.astype(F32)
    raw_two = jnp.concatenate([raw_hi, raw_lo], axis=0).astype(BF16)
    gp_all = dot_lanes(raw_two, act_buf[...])
    gp_all = gp_all[0:8] + gp_all[8:16]
    gp = gp_all[:, :feat] + gp_all[:, feat : 2 * feat]
    gp_buf[...] = gp[0:chans] * (1.0 / math.sqrt(seq_total))
    others(lambda peer: push(gp_buf, gp_in.at[me], 4, peer, my_tp))

    turned_params = jnp.transpose(params)[:feat]
    pt_hi, pt_lo = split(turned_params)
    pt_hi = pt_hi.astype(F32)
    pt_lo = pt_lo.astype(F32)
    pt_stack = jnp.concatenate([pt_hi, pt_lo, pt_hi, pt_lo], axis=1).astype(BF16)
    raw_four = jnp.concatenate([raw_hi, raw_hi, raw_lo, raw_lo], axis=0).astype(BF16)
    grad_hidden = dot(pt_stack, raw_four) * cos_buf[...]
    gh_hi, gh_lo = split(grad_hidden)
    gh_stack = jnp.concatenate([gh_hi, gh_lo], axis=0)
    gb_all = dot_lanes(gh_stack, basis_ref[0 : 2 * BAND, :])
    gb_all = gb_all[:feat] + gb_all[feat:]
    gb = (gb_all[:, :BAND] + gb_all[:, BAND : 2 * BAND]) * math.sqrt(
        feat / (seq_total * tp_chans)
    )
    share = feat // ctx_size
    for target in range(ctx_size):
        part_buf[target] = gb[target * share : (target + 1) * share]
    all_others(lambda ctx, tp: push(part_buf.at[ctx], part_in.at[my_id], 5, ctx, tp))
    part_in[my_id] = part_buf[me]

    settle(part_in, recv_sems.at[5], all_size - 1)
    sum_buf[...] = jnp.sum(part_in[...], axis=0)
    others(lambda peer: push(sum_buf, sum_in.at[me], 6, peer, my_tp))

    gp_in[me] = gp_buf[...]
    sum_in[me] = sum_buf[...]
    mq_back[me] = mq_send[me]
    kv_back[me] = kv_send[me]
    settle(mq_back, recv_sems.at[2], ctx_size - 1)
    mq_out[...] = mq_back[...]
    settle(kv_back, recv_sems.at[3], ctx_size - 1)
    kv_out[...] = kv_back[...]
    settle(gp_in, recv_sems.at[4], ctx_size - 1)
    proj_out[...] = gp_in[...]
    settle(sum_in, recv_sems.at[6], ctx_size - 1)
    for source in range(ctx_size):
        basis_out[source * share : (source + 1) * share, :] = sum_in[source][:, :emb]

    settle(kv_in, send_sems.at[0], ctx_size - 1)
    settle(qg_in, send_sems.at[1], ctx_size - 1)
    settle(mq_back, send_sems.at[2], ctx_size - 1)
    settle(kv_back, send_sems.at[3], ctx_size - 1)
    settle(gp_in, send_sems.at[4], ctx_size - 1)
    settle(part_in, send_sems.at[5], all_size - 1)
    settle(sum_in, send_sems.at[6], ctx_size - 1)


def on_device(
    tables,
    query_in,
    key_in,
    value_in,
    short_kernel,
    basis_weight,
    basis_bias,
    filter_proj,
    decay_rate,
    skip_gain,
    grad_out,
):
    ctx_size = lax.axis_size("ctx")
    tp_size = lax.axis_size("tp")
    chan_local, num_tok = query_in.shape
    seq_total = num_tok * ctx_size
    chans = chan_local // ctx_size
    taps = short_kernel.shape[2]
    feat, emb = basis_weight.shape
    folds = num_tok // LANES
    slab = folds * chans
    blocks = seq_total // LANES
    rows = blocks * chans

    def packed(first, second):
        both = jnp.stack([first, second]).reshape(2, ctx_size, chans, folds, LANES)
        return both.transpose(1, 0, 3, 2, 4).reshape(ctx_size, 2, slab, LANES)

    def unpacked(both):
        wide = both.reshape(ctx_size, 2, folds, chans, LANES).transpose(1, 0, 3, 2, 4)
        wide = wide.reshape(2, chan_local, num_tok)
        return wide[0], wide[1]

    energy = jnp.expm1(-2.0 * decay_rate) / jnp.expm1(-2.0 * decay_rate / seq_total)
    params = jnp.concatenate(
        [
            filter_proj,
            short_kernel[0],
            short_kernel[1],
            short_kernel[2],
            decay_rate[:, None],
            (1.0 / jnp.sqrt(energy))[:, None],
            skip_gain[:, None],
        ],
        axis=1,
    )
    params = jnp.pad(params, ((0, 0), (0, LANES - params.shape[1])))
    params = params.reshape(ctx_size, chans, LANES)
    params = jnp.tile(params, (1, 8 // chans, 1))
    weight = jnp.concatenate([basis_weight, basis_bias[:, None]], axis=1)
    weight = jnp.pad(weight, ((0, 0), (0, BAND - emb - 1)))
    weight = jnp.pad(jnp.tile(weight, (1, 6)), ((0, 0), (0, 256 - 6 * BAND)))
    share = feat // ctx_size
    all_size = ctx_size * tp_size
    slabs = (ctx_size, 2, slab, LANES)
    dims = (ctx_size, tp_size, chans, seq_total, taps, feat, emb, chan_local * tp_size)
    vmem = pl.BlockSpec(memory_space=pltpu.VMEM)
    mq, kv, grad_proj, grad_basis = pl.pallas_call(
        functools.partial(mixer_kernel, dims),
        out_shape=(
            jax.ShapeDtypeStruct(slabs, BF16),
            jax.ShapeDtypeStruct(slabs, BF16),
            jax.ShapeDtypeStruct((ctx_size, chans, feat), F32),
            jax.ShapeDtypeStruct((feat, emb), F32),
        ),
        in_specs=[vmem] * (4 + len(tables)),
        out_specs=(vmem, vmem, vmem, vmem),
        scratch_shapes=[
            pltpu.VMEM(slabs, BF16),
            pltpu.VMEM(slabs, BF16),
            pltpu.VMEM(slabs, BF16),
            pltpu.VMEM(slabs, BF16),
            pltpu.VMEM(slabs, BF16),
            pltpu.VMEM(slabs, BF16),
            pltpu.VMEM((2 * feat, seq_total), BF16),
            pltpu.VMEM((feat, seq_total), F32),
            pltpu.VMEM((rows, LANES), F32),
            pltpu.VMEM((rows, LANES), F32),
            pltpu.VMEM((ctx_size, share, BAND), F32),
            pltpu.VMEM((all_size, share, BAND), F32),
            pltpu.VMEM((share, BAND), F32),
            pltpu.VMEM((ctx_size, share, BAND), F32),
            pltpu.VMEM((chans, feat), F32),
            pltpu.VMEM((ctx_size, chans, feat), F32),
            pltpu.SemaphoreType.DMA((7,)),
            pltpu.SemaphoreType.DMA((7,)),
        ],
        compiler_params=pltpu.CompilerParams(
            collective_id=0, has_side_effects=True, vmem_limit_bytes=56 * 1024 * 1024
        ),
    )(packed(key_in, value_in), packed(query_in, grad_out), params, weight, *tables)
    mixed, grad_query = unpacked(mq)
    grad_key, grad_value = unpacked(kv)
    return (
        mixed,
        grad_query,
        grad_key,
        grad_value,
        grad_proj.reshape(chan_local, feat),
        grad_basis,
    )


def solution(mesh):
    ctx_size = mesh.shape["ctx"]

    def whole(*args):
        chans = args[0].shape[0] // mesh.shape["tp"] // ctx_size
        num_freq = (args[4].shape[1] - 1) // 2
        tables = constant_tables(args[0].shape[1], chans, num_freq)
        tables = tuple(jnp.asarray(table) for table in tables)
        return jax.shard_map(
            on_device,
            mesh=mesh,
            in_specs=(
                (P(),) * len(tables),
                P("tp", "ctx"),
                P("tp", "ctx"),
                P("tp", "ctx"),
                P(None, "tp", None),
                P(),
                P(),
                P("tp", None),
                P("tp"),
                P("tp"),
                P("tp", "ctx"),
            ),
            out_specs=(
                P("tp", "ctx"),
                P("tp", "ctx"),
                P("tp", "ctx"),
                P("tp", "ctx"),
                P("tp", None),
                P(),
            ),
            check_vma=False,
        )(tables, *args)

    return whole
```

time: 201 us -> 47.1 us (0.23)
  blocking collectives: 100 us -> 0 us
  starting transfers between devices: 40.7 us -> 0 us
  Pallas kernels: 0 us -> 32.9 us
  matrix products: 24.1 us -> 0 us
  waiting for transfers between devices: 16.8 us -> 0 us
  other arithmetic: 10.7 us -> 3.07 us
  local copies, waits for them, and re-layouts: 6.19 us -> 9.82 us
    psum x2 -> x0, blocking collectives: 100 us -> none  [the longest x1 59.3 us: on_device(): grad_proj = lax.psum(part_proj, 'ctx') * proj_scale]
    pallas_call x0 -> x1, Pallas kernels: none -> 32.9 us  [on_device(): pl.pallas_call(functools.partial(mixer_kernel, dims), out_shape=(jax.Shap...]
    all_to_all x6 -> x0, starting transfers between devices: 28.2 us -> none  [the longest x1 7.35 us: on_device(): lax.all_to_all(filter_tok, 'ctx', split_axis=0, concat_axis=1, tiled=True)]
    dot_general x41 -> x0, matrix products: 24.1 us -> none  [the longest x3 2.61 us: restore(): jnp.einsum('kt,nks->nts', outer[1], turned_im, precision=PRECISE)]
    all_to_all x6 -> x0, waiting for transfers between devices: 14.8 us -> none  [the longest x1 6.63 us: on_device(): lax.all_to_all(carried_grad_chan, 'ctx', split_axis=1, concat_axis=0, til...]
    ppermute x6 -> x0, starting transfers between devices: 12.5 us -> none  [passed_along(): lax.ppermute(value, axis, [(source, source + steps) for source in range(l...]
    convert_element_type x15 -> x0, other arithmetic: 6.29 us -> none  [the longest x1 1.03 us: on_device(): featurize_back(grad_key_feat, following[1], short_kernel[1])]
    squeeze x1 -> x3, local copies, waits for them, and re-layouts: 0.01 us -> 3.79 us  [the longest x2 3.06 us: unpacked(): return (wide[0], wide[1])]
  transfers between devices with their start and end apart: 12 -> 0, of which waited for: 6 -> 0; matrix products, arithmetic and copies ran while one was open for 13% -> 0% of each run, Pallas kernels for 0% -> 0%
where the time goes in v1:
time: 47.1 us; the launch traced here: 46.5 us
  Pallas kernels  32.9 us (70%)
  local copies, waits for them, and re-layouts  9.82 us (21%)
  other arithmetic  3.07 us (7%)
  between operations  0.66 us (1%)
    pallas_call x1, Pallas kernels, on_device(): pl.pallas_call(functools.partial(mixer_kernel, dims), out_shape=(jax.Shap...  32.9 us
    unnamed x3, local copies, waits for them, and re-layouts  3.07 us
    squeeze x2, local copies, waits for them, and re-layouts, unpacked(): return (wide[0], wide[1])  3.06 us
    reshape x1, other arithmetic, packed(): return both.transpose(1, 0, 3, 2, 4).reshape(ctx_size, 2, slab, LANES)  1.65 us
    concatenate x1, local copies, waits for them, and re-layouts, on_device(): jnp.concatenate([filter_proj, short_kernel[0], short_kernel[1], short_ker...  1.59 us

profile of v1, /device:TPU:0, one launch (start us, length us, event | category | flops | bytes accessed | tf_op | source)
XLA Modules:
  0.0 46.5 jit_solution(10729695568141146435)
XLA Ops:
  0.6 0.7 %rsqrt_bitcast_fusion = f32[128,1]{0,1:T(1,128)S(1)} fusion(f32[128]{0:T(128)} %param.27), kind=kLoop, calls=%fused_computation.12 | loop fusion | flops 384 | bytes 1024 | tf_op jit(solution)/shard_map/broadcast_in_dim | solution.py:491
  1.3 0.7 %slice_bitcast_fusion.4 = (f32[128,7]{0,1:T(8,128)S(1)}, f32[128,7]{0,1:T(8,128)S(1)}, f32[128,7]{0,1:T(8,128)S(1)}) fusion(f32[3,128,7]{1,2,0:T(8,128)} %param.23), kind=kLoop, calls=%fused_computation.9 | loop fusion | bytes 21504 | tf_op jit(solution)/shard_map/squeeze | solution.py:489
  2.0 0.8 %select_maximum_fusion = f32[64,40]{0,1:T(8,128)S(1)} fusion(f32[64,1]{0,1:T(1,128)} %bitcast.59, f32[64,33]{0,1:T(8,128)} %param.24), kind=kLoop, calls=%fused_computation.7 | loop fusion | flops 10240 | bytes 18944 | tf_op jit(solution)/shard_map/concatenate | solution.py:499
  2.8 1.6 %concatenate.8 = f32[128,88]{0,1:T(8,128)S(1)} concatenate(f32[128,64]{0,1:T(8,128)} %param.26, f32[128,7]{0,1:T(8,128)S(1)} %get-tuple-element.31, f32[128,7]{0,1:T(8,128)S(1)} %get-tuple-element.32, f32[128,7]{0,1:T(8,128)S(1)} %get-tuple-element.30, f32[128,1]{0,1:T(1,128)} %bitcast.57, f32[128,1]{0,1:T(1,128)S(1)} %rsqrt_bitcast_fusion, f32[128,1]{0,1:T(1,128)} %bitcast.58), dimensions={1} | concatenate | bytes 90112 | tf_op jit(solution)/shard_map/concatenate | solution.py:484
  4.4 0.1 copy.42
  4.5 0.6 %pad_bitcast_fusion.params_ref = f32[16,8,128]{2,1,0:T(8,128)} fusion(f32[128,88]{1,0:T(8,128)S(1)} %copy.42), kind=kLoop, calls=%fused_computation.6 | loop fusion | bytes 110592 | tf_op jit(solution)/shard_map/tile;reshape | solution.py:498
  5.1 0.1 copy.39
  5.2 0.6 %pad.14.weight_ref = f32[64,256]{1,0:T(8,128)} pad(f32[64,240]{1,0:T(8,128)S(1)} %copy.39, f32[]{:T(128)} %constant.29.clone.1), padding=0_0x0_16 | pad | bytes 126980 | tf_op jit(solution)/shard_map/jit(_pad)/pad | solution.py:501
  5.9 1.6 %maximum_bitcast_fusion = (bf16[16,2,16,128]{3,2,1,0:T(8,128)(2,1)}, bf16[16,2,16,128]{3,2,1,0:T(8,128)(2,1)}) fusion(bf16[1,16,8,2,128]{4,2,3,0,1:T(8,128)(2,1)} %bitcast.53, bf16[1,16,8,2,128]{4,2,3,0,1:T(8,128)(2,1)} %bitcast.54, bf16[1,16,8,2,128]{4,2,3,0,1:T(8,128)(2,1)} %bitcast.55, bf16[1,16,8,2,128]{4,2,3,0,1:T(8,128)(2,1)} %bitcast.56), kind=kLoop, calls=%fused_computation | loop fusion | flops 131072 | bytes 524288 | tf_op jit(solution)/shard_map/reshape | solution.py:476
  7.5 32.9 %shard_map.235 = (bf16[16,2,16,128]{3,2,1,0:T(8,128)(2,1)}, bf16[16,2,16,128]{3,2,1,0:T(8,128)(2,1)}, f32[16,8,64]{2,1,0:T(8,128)}, f32[64,33]{1,0:T(8,128)}) custom-call(bf16[16,2,16,128]{3,2,1,0:T(8,128)(2,1)} %get-tuple-element.33.kv_ref, bf16[16,2,16,128]{3,2,1,0:T(8,128)(2,1)} %get-tuple-element.34.qg_ref, f32[16,8,128]{2,1,0:T(8,128)} %pad_bitcast_fusion.params_ref, ...), custom_call_target="tpu_custom_call" | custom-call | tf_op jit(solution)/shard_map/pallas_call | solution.py:507
  40.5 1.5 %slice_bitcast_fusion = (bf16[128,256]{1,0:T(8,128)(2,1)}, bf16[128,256]{1,0:T(8,128)(2,1)}) fusion(bf16[2,16,8,2,128]{4,2,3,0,1:T(8,128)(2,1)} %bitcast.51), kind=kLoop, calls=%fused_computation.2 | loop fusion | bytes 262144 | tf_op jit(solution)/shard_map/squeeze | solution.py:481
  42.0 1.5 %slice_bitcast_fusion.2 = (bf16[128,256]{1,0:T(8,128)(2,1)}, bf16[128,256]{1,0:T(8,128)(2,1)}) fusion(bf16[2,16,8,2,128]{4,2,3,0,1:T(8,128)(2,1)} %bitcast.50), kind=kLoop, calls=%fused_computation.4 | loop fusion | bytes 262144 | tf_op jit(solution)/shard_map/squeeze | solution.py:481
  43.5 1.4 %copy.41 = f32[64,33]{0,1:T(8,128)} copy(f32[64,33]{1,0:T(8,128)} %get-tuple-element.25) | data formatting | bytes 16896
  45.0 1.5 %copy.40 = f32[128,64]{0,1:T(8,128)} copy(f32[128,64]{1,0:T(8,128)} %bitcast.52) | data formatting | bytes 65536
  (1 shorter events, 0.0 us)

commit v2 on v1

--- a/solution.py
+++ b/solution.py
@@ -40,8 +40,13 @@
     back = np.zeros((2, spec_rows, blocks * chans))
     back[0, : kept * chans] = np.kron(weight * np.cos(turn), eye)
     back[1, : kept * chans] = np.kron(-weight * np.sin(turn), eye)
-    back = back.reshape(2 * spec_rows, blocks * chans).T.copy()
+    back = back.reshape(2 * spec_rows, blocks * chans)
     fwd = fwd.reshape(2 * spec_rows, blocks * chans)
+    if chans % 8 == 0:
+        used = np.r_[0:spec_rows, spec_rows + chans : 2 * spec_rows - chans]
+        back = back[used]
+        fwd = fwd[used]
+    back = back.T.copy()
     twist = 2.0 * np.pi * ((k1[:, None] * n2[None, :]) % (2 * seq_total)) / (2 * seq_total)
     twiddle = np.zeros((2, spec_rows, LANES))
     twiddle[0, : kept * chans] = np.repeat(np.cos(twist), chans, axis=0)
@@ -114,10 +119,30 @@
 
 def mixer_kernel(
     dims,
-    kv_ref,
-    qg_ref,
-    params_ref,
+    query_ref,
+    key_ref,
+    value_ref,
+    grad_ref,
+    taps_ref,
     weight_ref,
+    bias_ref,
+    proj_ref,
+    decay_ref,
+    skip_ref,
+    basis_hbm,
+    fwd_hi_hbm,
+    fwd_lo_hbm,
+    back_hi_hbm,
+    back_lo_hbm,
+    inner_hi_hbm,
+    inner_lo_hbm,
+    inv_hi_hbm,
+    inv_lo_hbm,
+    twiddle_hbm,
+    mq_out,
+    kv_out,
+    proj_out,
+    basis_out,
     basis_ref,
     fwd_hi,
     fwd_lo,
@@ -128,10 +153,11 @@
     inv_hi,
     inv_lo,
     twiddle_ref,
-    mq_out,
-    kv_out,
-    proj_out,
-    basis_out,
+    kv_ref,
+    qg_ref,
+    par_buf,
+    turn_buf,
+    wide_buf,
     kv_in,
     qg_in,
     mq_send,
@@ -150,6 +176,7 @@
     gp_in,
     send_sems,
     recv_sems,
+    table_sems,
 ):
     ctx_size, tp_size, chans, seq_total, taps, feat, emb, tp_chans = dims
     me = lax.axis_index("ctx")
@@ -157,7 +184,7 @@
     blocks = seq_total // LANES
     rows = blocks * chans
     spec_rows = twiddle_ref.shape[1]
-    slab = 2 * chans
+    slab = kv_ref.shape[2]
     all_size = ctx_size * tp_size
     my_id = my_tp * ctx_size + me
     chunk = 512
@@ -185,6 +212,42 @@
         )
 
     all_others(greet)
+
+    loads = [
+        pltpu.make_async_copy(source, target, table_sems.at[index])
+        for index, (source, target) in enumerate(
+            [
+                (basis_hbm, basis_ref),
+                (fwd_hi_hbm, fwd_hi),
+                (fwd_lo_hbm, fwd_lo),
+                (inner_hi_hbm, inner_hi),
+                (inner_lo_hbm, inner_lo),
+                (twiddle_hbm, twiddle_ref),
+                (inv_hi_hbm, inv_hi),
+                (inv_lo_hbm, inv_lo),
+                (back_hi_hbm, back_hi),
+                (back_lo_hbm, back_lo),
+            ]
+        )
+    ]
+    for load in loads:
+        load.start()
+
+    def pack(source, target, index):
+        wide = source[...].astype(F32)
+        for other in range(ctx_size):
+            target[other, index] = jnp.concatenate(
+                [
+                    wide[other * chans : (other + 1) * chans, fold * LANES : (fold + 1) * LANES]
+                    for fold in range(slab // chans)
+                ],
+                axis=0,
+            ).astype(BF16)
+
+    pack(key_ref, kv_ref, 0)
+    pack(value_ref, kv_ref, 1)
+    pack(query_ref, qg_ref, 0)
+    pack(grad_ref, qg_ref, 1)
     pl.semaphore_wait(barrier, all_size - 1)
 
     def push(src, dst, lane, ctx, tp):
@@ -206,23 +269,46 @@
     kv_in[me] = kv_ref[me]
     qg_in[me] = qg_ref[me]
 
-    params = params_ref[me]
+    def expm1(value):
+        series = 1.0 + value * (1.0 / 12.0)
+        for order in range(11, 1, -1):
+            series = 1.0 + value * series * (1.0 / order)
+        return jnp.where(value > -0.5, value * series, jnp.exp(value) - 1.0)
+
+    rates = decay_ref[...]
+    energy = expm1(-2.0 * rates) / expm1(-2.0 * rates / seq_total)
+    after = feat + 3 * taps
+    par_buf[...] = jnp.zeros_like(par_buf)
+    par_buf[0:feat] = proj_ref[...]
+    for which in range(3):
+        par_buf[feat + which * taps : feat + (which + 1) * taps] = taps_ref[which]
+    par_buf[after : after + 1] = rates
+    par_buf[after + 1 : after + 2] = 1.0 / jnp.sqrt(energy)
+    par_buf[after + 2 : after + 3] = skip_ref[...]
+    turn_buf[...] = jnp.transpose(par_buf[...])
+    params = turn_buf[pl.ds(pl.multiple_of(me * chans, chans), chans), :]
+    if chans < 8:
+        params = jnp.concatenate([params] * (8 // chans), axis=0)
 
     def column(index):
         wide = jnp.broadcast_to(params[:, index : index + 1], (8, LANES))
         return jnp.concatenate([wide] * (rows // 8), axis=0)
 
     tap_at = feat
-    decay = column(feat + 3 * taps)
-    inv_energy = column(feat + 3 * taps + 1)
-    skip = column(feat + 3 * taps + 2)
+    decay = column(after)
+    inv_energy = column(after + 1)
+    skip = column(after + 2)
 
     lane_ids = lax.broadcasted_iota(jnp.int32, (rows, LANES), 1)
     row_ids = lax.broadcasted_iota(jnp.int32, (rows, LANES), 0)
     positions = ((row_ids // chans) * LANES + lane_ids).astype(F32)
     envelope = jnp.exp(-(decay * positions) / seq_total) * inv_energy
 
-    weight = weight_ref[...]
+    wide_buf[...] = jnp.zeros_like(wide_buf)
+    wide_buf[0:emb, 0:feat] = weight_ref[...]
+    wide_buf[emb : emb + 1, 0:feat] = bias_ref[...]
+    weight = jnp.concatenate([wide_buf[...]] * 6 + [jnp.zeros((16, LANES), F32)], axis=0)
+    weight = jnp.transpose(weight)[0:feat]
     w_one = weight.astype(BF16)
     w_rest = weight - w_one.astype(F32)
     w_two = w_rest.astype(BF16)
@@ -264,12 +350,17 @@
             ]
         return carry
 
+    loads[0].wait()
     lax.fori_loop(0, seq_total // chunk, filter_step, 0)
     filt = (filt_buf[...] * envelope).astype(BF16)
+
+    blank = jnp.zeros((chans, LANES), F32)
 
     def spectrum(signal):
         outer = dot(fwd_hi[...], signal) + dot(fwd_lo[...], signal)
         out_re, out_im = outer[:spec_rows], outer[spec_rows:]
+        if chans % 8 == 0:
+            out_im = jnp.concatenate([blank, out_im, blank], axis=0)
         tw_re, tw_im = twiddle_ref[0], twiddle_ref[1]
         turned = jnp.concatenate(
             [out_re * tw_re - out_im * tw_im, out_re * tw_im + out_im * tw_re], axis=1
@@ -283,9 +374,10 @@
         section = dot(high, inv_hi[...]) + dot(high, inv_lo[...]) + dot(low, inv_hi[...])
         sec_re, sec_im = section[:, :LANES], section[:, LANES:]
         tw_re, tw_im = twiddle_ref[0], twiddle_ref[1]
-        turned = jnp.concatenate(
-            [sec_re * tw_re + sec_im * tw_im, sec_im * tw_re - sec_re * tw_im], axis=0
-        )
+        turn_im = sec_im * tw_re - sec_re * tw_im
+        if chans % 8 == 0:
+            turn_im = turn_im[chans : spec_rows - chans]
+        turned = jnp.concatenate([sec_re * tw_re + sec_im * tw_im, turn_im], axis=0)
         high, low = split(turned)
         return dot(back_hi[...], high) + dot(back_lo[...], high) + dot(back_hi[...], low)
 
@@ -304,8 +396,6 @@
             for target in range(ctx_size):
                 ref[target, index] = rows_buf[target * slab : (target + 1) * slab, :].astype(BF16)
 
-    blank = jnp.zeros((chans, LANES), F32)
-
     def down(value):
         if chans % 8 == 0:
             return jnp.concatenate([blank, value[: rows - chans]], axis=0)
@@ -332,6 +422,8 @@
             result = result + column(tap_at + which * taps + offset) * shifted
         return result
 
+    for load in loads[1:]:
+        load.wait()
     filt_re, filt_im = spectrum(filt)
 
     settle(kv_in, recv_sems.at[0], ctx_size - 1)
@@ -355,16 +447,6 @@
 
     grad_long = (grad_wide * query_feat).astype(BF16)
     grad_re, grad_im = spectrum(grad_long)
-
-    carried_grad = restore(
-        filt_re * grad_re + filt_im * grad_im, filt_re * grad_im - filt_im * grad_re
-    )
-    carried_grad = (carried_grad + skip * grad_long.astype(F32)).astype(BF16).astype(F32)
-    grad_key_feat = (carried_grad * value_feat).astype(BF16).astype(F32)
-    grad_value_feat = (carried_grad * key_feat).astype(BF16).astype(F32)
-    from_rows(kv_send, 0, featurize_back(grad_key_feat, 1).astype(BF16))
-    from_rows(kv_send, 1, featurize_back(grad_value_feat, 2).astype(BF16))
-    others(lambda peer: push(kv_send.at[peer], kv_back.at[me], 3, peer, my_tp))
 
     filter_grad = restore(
         carried_re * grad_re + carried_im * grad_im, carried_re * grad_im - carried_im * grad_re
@@ -395,7 +477,7 @@
     raw_two = jnp.concatenate([raw_hi, raw_lo], axis=0).astype(BF16)
     gp_all = dot_lanes(raw_two, act_buf[...])
     gp_all = gp_all[0:8] + gp_all[8:16]
-    gp = gp_all[:, :feat] + gp_all[:, feat : 2 * feat]
+    gp = gp_all + pltpu.roll(gp_all, feat, 1)
     gp_buf[...] = gp[0:chans] * (1.0 / math.sqrt(seq_total))
     others(lambda peer: push(gp_buf, gp_in.at[me], 4, peer, my_tp))
 
@@ -408,9 +490,9 @@
     grad_hidden = dot(pt_stack, raw_four) * cos_buf[...]
     gh_hi, gh_lo = split(grad_hidden)
     gh_stack = jnp.concatenate([gh_hi, gh_lo], axis=0)
-    gb_all = dot_lanes(gh_stack, basis_ref[0 : 2 * BAND, :])
+    gb_all = dot_lanes(gh_stack, basis_ref[0:LANES, :])
     gb_all = gb_all[:feat] + gb_all[feat:]
-    gb = (gb_all[:, :BAND] + gb_all[:, BAND : 2 * BAND]) * math.sqrt(
+    gb = (gb_all + pltpu.roll(gb_all, LANES - BAND, 1)) * math.sqrt(
         feat / (seq_total * tp_chans)
     )
     share = feat // ctx_size
@@ -418,6 +500,16 @@
         part_buf[target] = gb[target * share : (target + 1) * share]
     all_others(lambda ctx, tp: push(part_buf.at[ctx], part_in.at[my_id], 5, ctx, tp))
     part_in[my_id] = part_buf[me]
+
+    carried_grad = restore(
+        filt_re * grad_re + filt_im * grad_im, filt_re * grad_im - filt_im * grad_re
+    )
+    carried_grad = (carried_grad + skip * grad_long.astype(F32)).astype(BF16).astype(F32)
+    grad_key_feat = (carried_grad * value_feat).astype(BF16).astype(F32)
+    grad_value_feat = (carried_grad * key_feat).astype(BF16).astype(F32)
+    from_rows(kv_send, 0, featurize_back(grad_key_feat, 1).astype(BF16))
+    from_rows(kv_send, 1, featurize_back(grad_value_feat, 2).astype(BF16))
+    others(lambda peer: push(kv_send.at[peer], kv_back.at[me], 3, peer, my_tp))
 
     settle(part_in, recv_sems.at[5], all_size - 1)
     sum_buf[...] = jnp.sum(part_in[...], axis=0)
@@ -434,8 +526,7 @@
     settle(gp_in, recv_sems.at[4], ctx_size - 1)
     proj_out[...] = gp_in[...]
     settle(sum_in, recv_sems.at[6], ctx_size - 1)
-    for source in range(ctx_size):
-        basis_out[source * share : (source + 1) * share, :] = sum_in[source][:, :emb]
+    basis_out[...] = sum_in[...]
 
     settle(kv_in, send_sems.at[0], ctx_size - 1)
     settle(qg_in, send_sems.at[1], ctx_size - 1)
@@ -444,6 +535,42 @@
     settle(gp_in, send_sems.at[4], ctx_size - 1)
     settle(part_in, send_sems.at[5], all_size - 1)
     settle(sum_in, send_sems.at[6], ctx_size - 1)
+
+
+def unpack_kernel(
+    dims,
+    mq_ref,
+    kv_ref,
+    proj_ref,
+    basis_ref,
+    mixed_out,
+    query_out,
+    key_out,
+    value_out,
+    proj_out,
+    basis_out,
+):
+    ctx_size, chans, folds, share = dims
+    feat = ctx_size * share
+    group = max(1, 16 // chans)
+    for source, index, target in (
+        (mq_ref, 0, mixed_out),
+        (mq_ref, 1, query_out),
+        (kv_ref, 0, key_out),
+        (kv_ref, 1, value_out),
+    ):
+        for first in range(0, ctx_size, group):
+            pieces = [source[first + other, index].astype(F32) for other in range(group)]
+            for fold in range(folds):
+                target[
+                    first * chans : (first + group) * chans, fold * LANES : (fold + 1) * LANES
+                ] = jnp.concatenate(
+                    [piece[fold * chans : (fold + 1) * chans] for piece in pieces], axis=0
+                ).astype(BF16)
+    proj = jnp.concatenate([proj_ref[source] for source in range(ctx_size)], axis=0)
+    proj_out[...] = jnp.transpose(proj)[:feat]
+    basis = jnp.concatenate([basis_ref[source] for source in range(ctx_size)], axis=0)
+    basis_out[...] = jnp.transpose(basis)[: basis_out.shape[0]]
 
 
 def on_device(
@@ -471,50 +598,29 @@
     blocks = seq_total // LANES
     rows = blocks * chans
 
-    def packed(first, second):
-        both = jnp.stack([first, second]).reshape(2, ctx_size, chans, folds, LANES)
-        return both.transpose(1, 0, 3, 2, 4).reshape(ctx_size, 2, slab, LANES)
-
-    def unpacked(both):
-        wide = both.reshape(ctx_size, 2, folds, chans, LANES).transpose(1, 0, 3, 2, 4)
-        wide = wide.reshape(2, chan_local, num_tok)
-        return wide[0], wide[1]
-
-    energy = jnp.expm1(-2.0 * decay_rate) / jnp.expm1(-2.0 * decay_rate / seq_total)
-    params = jnp.concatenate(
-        [
-            filter_proj,
-            short_kernel[0],
-            short_kernel[1],
-            short_kernel[2],
-            decay_rate[:, None],
-            (1.0 / jnp.sqrt(energy))[:, None],
-            skip_gain[:, None],
-        ],
-        axis=1,
-    )
-    params = jnp.pad(params, ((0, 0), (0, LANES - params.shape[1])))
-    params = params.reshape(ctx_size, chans, LANES)
-    params = jnp.tile(params, (1, 8 // chans, 1))
-    weight = jnp.concatenate([basis_weight, basis_bias[:, None]], axis=1)
-    weight = jnp.pad(weight, ((0, 0), (0, BAND - emb - 1)))
-    weight = jnp.pad(jnp.tile(weight, (1, 6)), ((0, 0), (0, 256 - 6 * BAND)))
     share = feat // ctx_size
     all_size = ctx_size * tp_size
     slabs = (ctx_size, 2, slab, LANES)
     dims = (ctx_size, tp_size, chans, seq_total, taps, feat, emb, chan_local * tp_size)
     vmem = pl.BlockSpec(memory_space=pltpu.VMEM)
-    mq, kv, grad_proj, grad_basis = pl.pallas_call(
+    anywhere = pl.BlockSpec(memory_space=pl.ANY)
+    landed = pl.pallas_call(
         functools.partial(mixer_kernel, dims),
         out_shape=(
             jax.ShapeDtypeStruct(slabs, BF16),
             jax.ShapeDtypeStruct(slabs, BF16),
-            jax.ShapeDtypeStruct((ctx_size, chans, feat), F32),
-            jax.ShapeDtypeStruct((feat, emb), F32),
+            jax.ShapeDtypeStruct((ctx_size, chans, LANES), F32),
+            jax.ShapeDtypeStruct((ctx_size, share, LANES), F32),
         ),
-        in_specs=[vmem] * (4 + len(tables)),
+        in_specs=[vmem] * 10 + [anywhere] * len(tables),
         out_specs=(vmem, vmem, vmem, vmem),
-        scratch_shapes=[
+        scratch_shapes=[pltpu.VMEM(table.shape, table.dtype) for table in tables]
+        + [
+            pltpu.VMEM(slabs, BF16),
+            pltpu.VMEM(slabs, BF16),
+            pltpu.VMEM((LANES, chan_local), F32),
+            pltpu.VMEM((chan_local, LANES), F32),
+            pltpu.VMEM((BAND, LANES), F32),
             pltpu.VMEM(slabs, BF16),
             pltpu.VMEM(slabs, BF16),
             pltpu.VMEM(slabs, BF16),
@@ -525,29 +631,47 @@
             pltpu.VMEM((feat, seq_total), F32),
             pltpu.VMEM((rows, LANES), F32),
             pltpu.VMEM((rows, LANES), F32),
-            pltpu.VMEM((ctx_size, share, BAND), F32),
-            pltpu.VMEM((all_size, share, BAND), F32),
-            pltpu.VMEM((share, BAND), F32),
-            pltpu.VMEM((ctx_size, share, BAND), F32),
-            pltpu.VMEM((chans, feat), F32),
-            pltpu.VMEM((ctx_size, chans, feat), F32),
+            pltpu.VMEM((ctx_size, share, LANES), F32),
+            pltpu.VMEM((all_size, share, LANES), F32),
+            pltpu.VMEM((share, LANES), F32),
+            pltpu.VMEM((ctx_size, share, LANES), F32),
+            pltpu.VMEM((chans, LANES), F32),
+            pltpu.VMEM((ctx_size, chans, LANES), F32),
             pltpu.SemaphoreType.DMA((7,)),
             pltpu.SemaphoreType.DMA((7,)),
+            pltpu.SemaphoreType.DMA((len(tables),)),
         ],
         compiler_params=pltpu.CompilerParams(
             collective_id=0, has_side_effects=True, vmem_limit_bytes=56 * 1024 * 1024
         ),
-    )(packed(key_in, value_in), packed(query_in, grad_out), params, weight, *tables)
-    mixed, grad_query = unpacked(mq)
-    grad_key, grad_value = unpacked(kv)
-    return (
-        mixed,
-        grad_query,
-        grad_key,
-        grad_value,
-        grad_proj.reshape(chan_local, feat),
-        grad_basis,
+    )(
+        query_in,
+        key_in,
+        value_in,
+        grad_out,
+        short_kernel.transpose(0, 2, 1),
+        basis_weight.T,
+        basis_bias[None, :],
+        filter_proj.T,
+        decay_rate[None, :],
+        skip_gain[None, :],
+        *tables,
     )
+    block = jax.ShapeDtypeStruct((chan_local, num_tok), BF16)
+    mixed, grad_query, grad_key, grad_value, proj_turned, basis_turned = pl.pallas_call(
+        functools.partial(unpack_kernel, (ctx_size, chans, folds, share)),
+        out_shape=(
+            block,
+            block,
+            block,
+            block,
+            jax.ShapeDtypeStruct((feat, chan_local), F32),
+            jax.ShapeDtypeStruct((emb, feat), F32),
+        ),
+        in_specs=[vmem] * 4,
+        out_specs=(vmem,) * 6,
+    )(*landed)
+    return (mixed, grad_query, grad_key, grad_value, proj_turned.T, basis_turned.T)
 
 
 def solution(mesh):

time: 47.1 us -> 33.4 us (0.71)
  local copies, waits for them, and re-layouts: 9.82 us -> 0 us
  other arithmetic: 3.07 us -> 0 us
    squeeze x3 -> x0, local copies, waits for them, and re-layouts: 3.79 us -> none  [the longest x2 3.06 us: unpacked(): return (wide[0], wide[1])]
    unnamed x3 -> x0, local copies, waits for them, and re-layouts: 3.07 us -> none
    pallas_call x1, Pallas kernels: 32.9 us -> 30.9 us  [on_device(): pl.pallas_call(functools.partial(mixer_kernel, dims), out_shape=(jax.Shap...]
    pallas_call x0 -> x1, Pallas kernels: none -> 1.7 us  [on_device(): pl.pallas_call(functools.partial(unpack_kernel, (ctx_size, chans, folds,...]
    reshape x1 -> x0, other arithmetic: 1.65 us -> none  [packed(): return both.transpose(1, 0, 3, 2, 4).reshape(ctx_size, 2, slab, LANES)]
    concatenate x1 -> x0, local copies, waits for them, and re-layouts: 1.59 us -> none  [on_device(): jnp.concatenate([filter_proj, short_kernel[0], short_kernel[1], short_ker...]
    concatenate x1 -> x0, other arithmetic: 0.75 us -> none  [on_device(): weight = jnp.concatenate([basis_weight, basis_bias[:, None]], axis=1)]
    another operation x3 -> x0, local copies, waits for them, and re-layouts: 0.73 us -> none  [the longest x1 0.64 us: on_device(): params = jnp.tile(params, (1, 8 // chans, 1))]
where the time goes in v2:
time: 33.4 us; the launch traced here: 33.2 us
  Pallas kernels  32.6 us (98%)
  between operations  0.64 us (2%)
    pallas_call x1, Pallas kernels, on_device(): pl.pallas_call(functools.partial(mixer_kernel, dims), out_shape=(jax.Shap...  30.9 us
    pallas_call x1, Pallas kernels, on_device(): pl.pallas_call(functools.partial(unpack_kernel, (ctx_size, chans, folds,...  1.7 us

profile of v2, /device:TPU:0, one launch (start us, length us, event | category | flops | bytes accessed | tf_op | source)
XLA Modules:
  0.0 33.2 jit_solution(7105473694869472305)
XLA Ops:
  0.6 30.9 %shard_map.235 = (bf16[16,2,16,128]{3,2,1,0:T(8,128)(2,1)}, bf16[16,2,16,128]{3,2,1,0:T(8,128)(2,1)}, f32[16,8,128]{2,1,0:T(8,128)}, f32[16,4,128]{2,1,0:T(4,128)}) custom-call(bf16[128,256]{1,0:T(8,128)(2,1)} %query_ref.1, bf16[128,256]{1,0:T(8,128)(2,1)} %key_ref.1, bf16[128,256]{1,0:T(8,128)(2,1)} %value_ref.1, bf16[128,256]{1,0:T(8,128)(2,1)} %grad_ref.1, ...), custom_call_target="tpu_custom_call" | custom-call | tf_op jit(solution)/shard_map/pallas_call | solution.py:607
  31.5 1.7 %shard_map.236 = (bf16[128,256]{1,0:T(8,128)(2,1)}, bf16[128,256]{1,0:T(8,128)(2,1)}, bf16[128,256]{1,0:T(8,128)(2,1)}, bf16[128,256]{1,0:T(8,128)(2,1)}, f32[64,128]{1,0:T(8,128)}, /*index=5*/f32[33,64]{1,0:T(8,128)}) custom-call(bf16[16,2,16,128]{3,2,1,0:T(8,128)(2,1)} %get-tuple-element.16.mq_ref, bf16[16,2,16,128]{3,2,1,0:T(8,128)(2,1)} %get-tuple-element.17.kv_ref, ...), custom_call_target="tpu_custom_call" | custom-call | tf_op jit(solution)/shard_map/pallas_call | solution.py:661

commit v3 on v2

--- a/solution.py
+++ b/solution.py
@@ -153,13 +153,11 @@
     inv_hi,
     inv_lo,
     twiddle_ref,
-    kv_ref,
-    qg_ref,
+    raw_ref,
     par_buf,
     turn_buf,
     wide_buf,
-    kv_in,
-    qg_in,
+    raw_in,
     mq_send,
     kv_send,
     mq_back,
@@ -170,10 +168,9 @@
     rows_buf,
     part_buf,
     part_in,
+    half_buf,
     sum_buf,
     sum_in,
-    gp_buf,
-    gp_in,
     send_sems,
     recv_sems,
     table_sems,
@@ -184,25 +181,26 @@
     blocks = seq_total // LANES
     rows = blocks * chans
     spec_rows = twiddle_ref.shape[1]
-    slab = kv_ref.shape[2]
-    all_size = ctx_size * tp_size
-    my_id = my_tp * ctx_size + me
+    slab = raw_ref.shape[2]
     chunk = 512
 
+    def around(axis_size, own, body):
+        def step(offset, carry):
+            other = own + offset
+            body(jnp.where(other >= axis_size, other - axis_size, other))
+            return carry
+
+        if axis_size <= 16:
+            for offset in range(1, axis_size):
+                step(offset, 0)
+        else:
+            lax.fori_loop(1, axis_size, step, 0)
+
     def others(body):
-        def step(offset, carry):
-            body(lax.rem(me + offset, ctx_size))
-            return carry
-
-        lax.fori_loop(1, ctx_size, step, 0)
-
-    def all_others(body):
-        def step(offset, carry):
-            other = lax.rem(my_id + offset, all_size)
-            body(lax.rem(other, ctx_size), other // ctx_size)
-            return carry
-
-        lax.fori_loop(1, all_size, step, 0)
+        around(ctx_size, me, body)
+
+    def tp_others(body):
+        around(tp_size, my_tp, body)
 
     barrier = pltpu.get_barrier_semaphore()
 
@@ -211,7 +209,8 @@
             barrier, inc=1, device_id={"ctx": ctx, "tp": tp}, device_id_type=MESH
         )
 
-    all_others(greet)
+    others(lambda peer: greet(peer, my_tp))
+    tp_others(lambda peer: greet(me, peer))
 
     loads = [
         pltpu.make_async_copy(source, target, table_sems.at[index])
@@ -244,11 +243,11 @@
                 axis=0,
             ).astype(BF16)
 
-    pack(key_ref, kv_ref, 0)
-    pack(value_ref, kv_ref, 1)
-    pack(query_ref, qg_ref, 0)
-    pack(grad_ref, qg_ref, 1)
-    pl.semaphore_wait(barrier, all_size - 1)
+    pack(key_ref, raw_ref, 0)
+    pack(value_ref, raw_ref, 1)
+    pack(query_ref, raw_ref, 2)
+    pack(grad_ref, raw_ref, 3)
+    pl.semaphore_wait(barrier, ctx_size + tp_size - 2)
 
     def push(src, dst, lane, ctx, tp):
         pltpu.make_async_remote_copy(
@@ -264,10 +263,8 @@
         part = ref.at[pl.ds(0, count)]
         pltpu.make_async_copy(part, part, sem).wait()
 
-    others(lambda peer: push(kv_ref.at[peer], kv_in.at[me], 0, peer, my_tp))
-    others(lambda peer: push(qg_ref.at[peer], qg_in.at[me], 1, peer, my_tp))
-    kv_in[me] = kv_ref[me]
-    qg_in[me] = qg_ref[me]
+    others(lambda peer: push(raw_ref.at[peer], raw_in.at[me], 0, peer, my_tp))
+    raw_in[me] = raw_ref[me]
 
     def expm1(value):
         series = 1.0 + value * (1.0 / 12.0)
@@ -356,18 +353,31 @@
 
     blank = jnp.zeros((chans, LANES), F32)
 
-    def spectrum(signal):
-        outer = dot(fwd_hi[...], signal) + dot(fwd_lo[...], signal)
-        out_re, out_im = outer[:spec_rows], outer[spec_rows:]
-        if chans % 8 == 0:
-            out_im = jnp.concatenate([blank, out_im, blank], axis=0)
+    def spectra(signals):
+        count = len(signals)
+        both = jnp.concatenate(signals, axis=1) if count > 1 else signals[0]
+        outer = dot(fwd_hi[...], both) + dot(fwd_lo[...], both)
         tw_re, tw_im = twiddle_ref[0], twiddle_ref[1]
-        turned = jnp.concatenate(
-            [out_re * tw_re - out_im * tw_im, out_re * tw_im + out_im * tw_re], axis=1
-        )
-        high, low = split(turned)
+        turned = []
+        for index in range(count):
+            own = outer[:, index * LANES : (index + 1) * LANES]
+            out_re, out_im = own[:spec_rows], own[spec_rows:]
+            if chans % 8 == 0:
+                out_im = jnp.concatenate([blank, out_im, blank], axis=0)
+            turned.append(
+                jnp.concatenate(
+                    [out_re * tw_re - out_im * tw_im, out_re * tw_im + out_im * tw_re], axis=1
+                )
+            )
+        high, low = split(jnp.concatenate(turned, axis=0) if count > 1 else turned[0])
         spec = dot(high, inner_hi[...]) + dot(high, inner_lo[...]) + dot(low, inner_hi[...])
-        return spec[:, :LANES], spec[:, LANES:]
+        return [
+            (
+                spec[index * spec_rows : (index + 1) * spec_rows, :LANES],
+                spec[index * spec_rows : (index + 1) * spec_rows, LANES:],
+            )
+            for index in range(count)
+        ]
 
     def restore(spec_re, spec_im):
         high, low = split(jnp.concatenate([spec_re, spec_im], axis=1))
@@ -379,7 +389,8 @@
             turn_im = turn_im[chans : spec_rows - chans]
         turned = jnp.concatenate([sec_re * tw_re + sec_im * tw_im, turn_im], axis=0)
         high, low = split(turned)
-        return dot(back_hi[...], high) + dot(back_lo[...], high) + dot(back_hi[...], low)
+        pair = dot(back_hi[...], jnp.concatenate([high, low], axis=1))
+        return pair[:, :LANES] + pair[:, LANES:] + dot(back_lo[...], high)
 
     def to_rows(ref, index):
         if slab % 16 == 0:
@@ -424,29 +435,26 @@
 
     for load in loads[1:]:
         load.wait()
-    filt_re, filt_im = spectrum(filt)
-
-    settle(kv_in, recv_sems.at[0], ctx_size - 1)
-    key_feat = featurize(to_rows(kv_in, 0), 1)
-    value_feat = featurize(to_rows(kv_in, 1), 2)
+    ((filt_re, filt_im),) = spectra([filt])
+
+    settle(raw_in, recv_sems.at[0], ctx_size - 1)
+    key_feat = featurize(to_rows(raw_in, 0), 1)
+    value_feat = featurize(to_rows(raw_in, 1), 2)
+    query_feat = featurize(to_rows(raw_in, 2), 0)
+    grad_wide = to_rows(raw_in, 3)
     carried = (key_feat * value_feat).astype(BF16)
-    carried_re, carried_im = spectrum(carried)
+    grad_long = (grad_wide * query_feat).astype(BF16)
+    (carried_re, carried_im), (grad_re, grad_im) = spectra([carried, grad_long])
 
     long_out = restore(
         filt_re * carried_re - filt_im * carried_im, filt_re * carried_im + filt_im * carried_re
     )
     long_out = (long_out + skip * carried.astype(F32)).astype(BF16).astype(F32)
 
-    settle(qg_in, recv_sems.at[1], ctx_size - 1)
-    query_feat = featurize(to_rows(qg_in, 0), 0)
-    grad_wide = to_rows(qg_in, 1)
     from_rows(mq_send, 0, (query_feat * long_out).astype(BF16))
     grad_query_feat = (grad_wide * long_out).astype(BF16).astype(F32)
     from_rows(mq_send, 1, featurize_back(grad_query_feat, 0).astype(BF16))
     others(lambda peer: push(mq_send.at[peer], mq_back.at[me], 2, peer, my_tp))
-
-    grad_long = (grad_wide * query_feat).astype(BF16)
-    grad_re, grad_im = spectrum(grad_long)
 
     filter_grad = restore(
         carried_re * grad_re + carried_im * grad_im, carried_re * grad_im - carried_im * grad_re
@@ -478,8 +486,7 @@
     gp_all = dot_lanes(raw_two, act_buf[...])
     gp_all = gp_all[0:8] + gp_all[8:16]
     gp = gp_all + pltpu.roll(gp_all, feat, 1)
-    gp_buf[...] = gp[0:chans] * (1.0 / math.sqrt(seq_total))
-    others(lambda peer: push(gp_buf, gp_in.at[me], 4, peer, my_tp))
+    gp = gp[0:chans] * (1.0 / math.sqrt(seq_total))
 
     turned_params = jnp.transpose(params)[:feat]
     pt_hi, pt_lo = split(turned_params)
@@ -497,9 +504,10 @@
     )
     share = feat // ctx_size
     for target in range(ctx_size):
-        part_buf[target] = gb[target * share : (target + 1) * share]
-    all_others(lambda ctx, tp: push(part_buf.at[ctx], part_in.at[my_id], 5, ctx, tp))
-    part_in[my_id] = part_buf[me]
+        part_buf[target, 0:chans] = gp
+        part_buf[target, chans : chans + share] = gb[target * share : (target + 1) * share]
+    others(lambda peer: push(part_buf.at[peer], part_in.at[me], 1, peer, my_tp))
+    part_in[me] = part_buf[me]
 
     carried_grad = restore(
         filt_re * grad_re + filt_im * grad_im, filt_re * grad_im - filt_im * grad_re
@@ -509,32 +517,31 @@
     grad_value_feat = (carried_grad * key_feat).astype(BF16).astype(F32)
     from_rows(kv_send, 0, featurize_back(grad_key_feat, 1).astype(BF16))
     from_rows(kv_send, 1, featurize_back(grad_value_feat, 2).astype(BF16))
+    settle(part_in, recv_sems.at[1], ctx_size - 1)
+    half_buf[my_tp] = jnp.sum(part_in[:, chans : chans + share], axis=0)
+    tp_others(lambda peer: push(half_buf.at[my_tp], half_buf.at[my_tp], 4, me, peer))
     others(lambda peer: push(kv_send.at[peer], kv_back.at[me], 3, peer, my_tp))
 
-    settle(part_in, recv_sems.at[5], all_size - 1)
-    sum_buf[...] = jnp.sum(part_in[...], axis=0)
-    others(lambda peer: push(sum_buf, sum_in.at[me], 6, peer, my_tp))
-
-    gp_in[me] = gp_buf[...]
+    settle(half_buf, recv_sems.at[4], tp_size - 1)
+    sum_buf[...] = jnp.sum(half_buf[...], axis=0)
+    others(lambda peer: push(sum_buf, sum_in.at[me], 5, peer, my_tp))
     sum_in[me] = sum_buf[...]
     mq_back[me] = mq_send[me]
     kv_back[me] = kv_send[me]
+    proj_out[...] = part_in[:, 0:chans]
     settle(mq_back, recv_sems.at[2], ctx_size - 1)
     mq_out[...] = mq_back[...]
     settle(kv_back, recv_sems.at[3], ctx_size - 1)
     kv_out[...] = kv_back[...]
-    settle(gp_in, recv_sems.at[4], ctx_size - 1)
-    proj_out[...] = gp_in[...]
-    settle(sum_in, recv_sems.at[6], ctx_size - 1)
+    settle(sum_in, recv_sems.at[5], ctx_size - 1)
     basis_out[...] = sum_in[...]
 
-    settle(kv_in, send_sems.at[0], ctx_size - 1)
-    settle(qg_in, send_sems.at[1], ctx_size - 1)
+    settle(raw_in, send_sems.at[0], ctx_size - 1)
+    settle(part_in, send_sems.at[1], ctx_size - 1)
     settle(mq_back, send_sems.at[2], ctx_size - 1)
     settle(kv_back, send_sems.at[3], ctx_size - 1)
-    settle(gp_in, send_sems.at[4], ctx_size - 1)
-    settle(part_in, send_sems.at[5], all_size - 1)
-    settle(sum_in, send_sems.at[6], ctx_size - 1)
+    settle(half_buf, send_sems.at[4], tp_size - 1)
+    settle(sum_in, send_sems.at[5], ctx_size - 1)
 
 
 def unpack_kernel(
@@ -599,7 +606,7 @@
     rows = blocks * chans
 
     share = feat // ctx_size
-    all_size = ctx_size * tp_size
+    raw_slabs = (ctx_size, 4, slab, LANES)
     slabs = (ctx_size, 2, slab, LANES)
     dims = (ctx_size, tp_size, chans, seq_total, taps, feat, emb, chan_local * tp_size)
     vmem = pl.BlockSpec(memory_space=pltpu.VMEM)
@@ -616,13 +623,11 @@
         out_specs=(vmem, vmem, vmem, vmem),
         scratch_shapes=[pltpu.VMEM(table.shape, table.dtype) for table in tables]
         + [
-            pltpu.VMEM(slabs, BF16),
-            pltpu.VMEM(slabs, BF16),
+            pltpu.VMEM(raw_slabs, BF16),
             pltpu.VMEM((LANES, chan_local), F32),
             pltpu.VMEM((chan_local, LANES), F32),
             pltpu.VMEM((BAND, LANES), F32),
-            pltpu.VMEM(slabs, BF16),
-            pltpu.VMEM(slabs, BF16),
+            pltpu.VMEM(raw_slabs, BF16),
             pltpu.VMEM(slabs, BF16),
             pltpu.VMEM(slabs, BF16),
             pltpu.VMEM(slabs, BF16),
@@ -631,14 +636,13 @@
             pltpu.VMEM((feat, seq_total), F32),
             pltpu.VMEM((rows, LANES), F32),
             pltpu.VMEM((rows, LANES), F32),
-            pltpu.VMEM((ctx_size, share, LANES), F32),
-            pltpu.VMEM((all_size, share, LANES), F32),
+            pltpu.VMEM((ctx_size, chans + share, LANES), F32),
+            pltpu.VMEM((ctx_size, chans + share, LANES), F32),
+            pltpu.VMEM((tp_size, share, LANES), F32),
             pltpu.VMEM((share, LANES), F32),
             pltpu.VMEM((ctx_size, share, LANES), F32),
-            pltpu.VMEM((chans, LANES), F32),
-            pltpu.VMEM((ctx_size, chans, LANES), F32),
-            pltpu.SemaphoreType.DMA((7,)),
-            pltpu.SemaphoreType.DMA((7,)),
+            pltpu.SemaphoreType.DMA((6,)),
+            pltpu.SemaphoreType.DMA((6,)),
             pltpu.SemaphoreType.DMA((len(tables),)),
         ],
         compiler_params=pltpu.CompilerParams(

time: 33.4 us -> 33.6 us (level)
  no operation moved by 1% of the time
where the time goes in v3:
time: 33.6 us; the launch traced here: 33.4 us
  Pallas kernels  32.7 us (97%)
  between operations  0.64 us (2%)
    pallas_call x1, Pallas kernels, on_device(): pl.pallas_call(functools.partial(mixer_kernel, dims), out_shape=(jax.Shap...  31 us
    pallas_call x1, Pallas kernels, on_device(): pl.pallas_call(functools.partial(unpack_kernel, (ctx_size, chans, folds,...  1.7 us

profile of v3, /device:TPU:0, one launch (start us, length us, event | category | flops | bytes accessed | tf_op | source)
XLA Modules:
  0.0 33.4 jit_solution(1260014353794610962)
XLA Ops:
  0.6 31.0 %shard_map.235 = (bf16[16,2,16,128]{3,2,1,0:T(8,128)(2,1)}, bf16[16,2,16,128]{3,2,1,0:T(8,128)(2,1)}, f32[16,8,128]{2,1,0:T(8,128)}, f32[16,4,128]{2,1,0:T(4,128)}) custom-call(bf16[128,256]{1,0:T(8,128)(2,1)} %query_ref.1, bf16[128,256]{1,0:T(8,128)(2,1)} %key_ref.1, bf16[128,256]{1,0:T(8,128)(2,1)} %value_ref.1, bf16[128,256]{1,0:T(8,128)(2,1)} %grad_ref.1, ...), custom_call_target="tpu_custom_call" | custom-call | tf_op jit(solution)/shard_map/pallas_call | solution.py:614
  31.7 1.7 %shard_map.236 = (bf16[128,256]{1,0:T(8,128)(2,1)}, bf16[128,256]{1,0:T(8,128)(2,1)}, bf16[128,256]{1,0:T(8,128)(2,1)}, bf16[128,256]{1,0:T(8,128)(2,1)}, f32[64,128]{1,0:T(8,128)}, /*index=5*/f32[33,64]{1,0:T(8,128)}) custom-call(bf16[16,2,16,128]{3,2,1,0:T(8,128)(2,1)} %get-tuple-element.16.mq_ref, bf16[16,2,16,128]{3,2,1,0:T(8,128)(2,1)} %get-tuple-element.17.kv_ref, ...), custom_call_target="tpu_custom_call" | custom-call | tf_op jit(solution)/shard_map/pallas_call | solution.py:665

commit v4 on v3

--- a/solution.py
+++ b/solution.py
@@ -69,12 +69,14 @@
     third = (rest - second.astype(np.float64)).astype(ml_dtypes.bfloat16)
     rim = np.zeros((16, seq_total), ml_dtypes.bfloat16)
     basis_table = np.concatenate([first, second, third, first, second, first, rim])
+    gap = np.zeros((LANES - 2 * BAND, seq_total), ml_dtypes.bfloat16)
     return (
         basis_table,
+        np.concatenate([first, second, gap]).T.copy(),
         *halves(fwd),
-        *halves(back),
-        *halves(inner),
-        *halves(inner_back),
+        back.astype(ml_dtypes.bfloat16),
+        inner.astype(ml_dtypes.bfloat16),
+        inner_back.astype(ml_dtypes.bfloat16),
         twiddle.astype(np.float32),
     )
 
@@ -130,28 +132,24 @@
     decay_ref,
     skip_ref,
     basis_hbm,
+    turned_hbm,
     fwd_hi_hbm,
     fwd_lo_hbm,
-    back_hi_hbm,
-    back_lo_hbm,
-    inner_hi_hbm,
-    inner_lo_hbm,
-    inv_hi_hbm,
-    inv_lo_hbm,
+    back_hbm,
+    inner_hbm,
+    inv_hbm,
     twiddle_hbm,
     mq_out,
     kv_out,
     proj_out,
     basis_out,
     basis_ref,
+    turned_ref,
     fwd_hi,
     fwd_lo,
-    back_hi,
-    back_lo,
-    inner_hi,
-    inner_lo,
-    inv_hi,
-    inv_lo,
+    back_ref,
+    inner_ref,
+    inv_ref,
     twiddle_ref,
     raw_ref,
     par_buf,
@@ -219,13 +217,11 @@
                 (basis_hbm, basis_ref),
                 (fwd_hi_hbm, fwd_hi),
                 (fwd_lo_hbm, fwd_lo),
-                (inner_hi_hbm, inner_hi),
-                (inner_lo_hbm, inner_lo),
+                (inner_hbm, inner_ref),
                 (twiddle_hbm, twiddle_ref),
-                (inv_hi_hbm, inv_hi),
-                (inv_lo_hbm, inv_lo),
-                (back_hi_hbm, back_hi),
-                (back_lo_hbm, back_lo),
+                (inv_hbm, inv_ref),
+                (back_hbm, back_ref),
+                (turned_hbm, turned_ref),
             ]
         )
     ]
@@ -329,15 +325,17 @@
         axis=0,
     ).astype(BF16)
 
-    def filter_step(index, carry):
-        start = pl.multiple_of(index * chunk, chunk)
-        here = pl.ds(start, chunk)
+    def activate(here):
         hidden = dot(w_stack, basis_ref[:, here])
         act, cosine = sine_cosine(hidden)
         cos_buf[:, here] = cosine
         act_hi, act_lo = split(act)
         act_buf[0:feat, here] = act_hi
         act_buf[feat : 2 * feat, here] = act_lo
+
+    def filter_step(index, carry):
+        here = pl.ds(pl.multiple_of(index * chunk, chunk), chunk)
+        activate(here)
         both = dot(proj_stack, act_buf[:, here])
         piece = both[0:8] + both[8:16]
         for block in range(chunk // LANES):
@@ -348,8 +346,18 @@
         return carry
 
     loads[0].wait()
-    lax.fori_loop(0, seq_total // chunk, filter_step, 0)
-    filt = (filt_buf[...] * envelope).astype(BF16)
+    if chans % 8 == 0:
+        for index in range(seq_total // chunk):
+            activate(pl.ds(index * chunk, chunk))
+        both = dot(proj_stack, act_buf[...])
+        piece = both[0:8] + both[8:16]
+        filt = jnp.concatenate(
+            [piece[:, block * LANES : (block + 1) * LANES] for block in range(blocks)], axis=0
+        )
+    else:
+        lax.fori_loop(0, seq_total // chunk, filter_step, 0)
+        filt = filt_buf[...]
+    filt = (filt * envelope).astype(BF16)
 
     blank = jnp.zeros((chans, LANES), F32)
 
@@ -370,7 +378,7 @@
                 )
             )
         high, low = split(jnp.concatenate(turned, axis=0) if count > 1 else turned[0])
-        spec = dot(high, inner_hi[...]) + dot(high, inner_lo[...]) + dot(low, inner_hi[...])
+        spec = dot(high, inner_ref[...]) + dot(low, inner_ref[...])
         return [
             (
                 spec[index * spec_rows : (index + 1) * spec_rows, :LANES],
@@ -381,7 +389,7 @@
 
     def restore(spec_re, spec_im):
         high, low = split(jnp.concatenate([spec_re, spec_im], axis=1))
-        section = dot(high, inv_hi[...]) + dot(high, inv_lo[...]) + dot(low, inv_hi[...])
+        section = dot(high, inv_ref[...]) + dot(low, inv_ref[...])
         sec_re, sec_im = section[:, :LANES], section[:, LANES:]
         tw_re, tw_im = twiddle_ref[0], twiddle_ref[1]
         turn_im = sec_im * tw_re - sec_re * tw_im
@@ -389,8 +397,8 @@
             turn_im = turn_im[chans : spec_rows - chans]
         turned = jnp.concatenate([sec_re * tw_re + sec_im * tw_im, turn_im], axis=0)
         high, low = split(turned)
-        pair = dot(back_hi[...], jnp.concatenate([high, low], axis=1))
-        return pair[:, :LANES] + pair[:, LANES:] + dot(back_lo[...], high)
+        pair = dot(back_ref[...], jnp.concatenate([high, low], axis=1))
+        return pair[:, :LANES] + pair[:, LANES:]
 
     def to_rows(ref, index):
         if slab % 16 == 0:
@@ -483,7 +491,7 @@
     raw_hi = raw_hi.astype(F32)
     raw_lo = raw_lo.astype(F32)
     raw_two = jnp.concatenate([raw_hi, raw_lo], axis=0).astype(BF16)
-    gp_all = dot_lanes(raw_two, act_buf[...])
+    gp_all = jnp.transpose(dot_lanes(act_buf[...], raw_two))
     gp_all = gp_all[0:8] + gp_all[8:16]
     gp = gp_all + pltpu.roll(gp_all, feat, 1)
     gp = gp[0:chans] * (1.0 / math.sqrt(seq_total))
@@ -497,7 +505,7 @@
     grad_hidden = dot(pt_stack, raw_four) * cos_buf[...]
     gh_hi, gh_lo = split(grad_hidden)
     gh_stack = jnp.concatenate([gh_hi, gh_lo], axis=0)
-    gb_all = dot_lanes(gh_stack, basis_ref[0:LANES, :])
+    gb_all = dot(gh_stack, turned_ref[...])
     gb_all = gb_all[:feat] + gb_all[feat:]
     gb = (gb_all + pltpu.roll(gb_all, LANES - BAND, 1)) * math.sqrt(
         feat / (seq_total * tp_chans)

time: 33.6 us -> 33.3 us (level)
  no operation moved by 1% of the time
where the time goes in v4:
time: 33.3 us; the launch traced here: 33.1 us
  Pallas kernels  32.5 us (98%)
  between operations  0.64 us (2%)
    pallas_call x1, Pallas kernels, on_device(): pl.pallas_call(functools.partial(mixer_kernel, dims), out_shape=(jax.Shap...  30.8 us
    pallas_call x1, Pallas kernels, on_device(): pl.pallas_call(functools.partial(unpack_kernel, (ctx_size, chans, folds,...  1.7 us

profile of v4, /device:TPU:0, one launch (start us, length us, event | category | flops | bytes accessed | tf_op | source)
XLA Modules:
  0.0 33.1 jit_solution(3661997314045973484)
XLA Ops:
  0.6 30.8 %shard_map.217 = (bf16[16,2,16,128]{3,2,1,0:T(8,128)(2,1)}, bf16[16,2,16,128]{3,2,1,0:T(8,128)(2,1)}, f32[16,8,128]{2,1,0:T(8,128)}, f32[16,4,128]{2,1,0:T(4,128)}) custom-call(bf16[128,256]{1,0:T(8,128)(2,1)} %query_ref.1, bf16[128,256]{1,0:T(8,128)(2,1)} %key_ref.1, bf16[128,256]{1,0:T(8,128)(2,1)} %value_ref.1, bf16[128,256]{1,0:T(8,128)(2,1)} %grad_ref.1, ...), custom_call_target="tpu_custom_call" | custom-call | tf_op jit(solution)/shard_map/pallas_call | solution.py:622
  31.4 1.7 %shard_map.218 = (bf16[128,256]{1,0:T(8,128)(2,1)}, bf16[128,256]{1,0:T(8,128)(2,1)}, bf16[128,256]{1,0:T(8,128)(2,1)}, bf16[128,256]{1,0:T(8,128)(2,1)}, f32[64,128]{1,0:T(8,128)}, /*index=5*/f32[33,64]{1,0:T(8,128)}) custom-call(bf16[16,2,16,128]{3,2,1,0:T(8,128)(2,1)} %get-tuple-element.16.mq_ref, bf16[16,2,16,128]{3,2,1,0:T(8,128)(2,1)} %get-tuple-element.17.kv_ref, ...), custom_call_target="tpu_custom_call" | custom-call | tf_op jit(solution)/shard_map/pallas_call | solution.py:673

commit v5 on v3

--- a/solution.py
+++ b/solution.py
@@ -69,8 +69,10 @@
     third = (rest - second.astype(np.float64)).astype(ml_dtypes.bfloat16)
     rim = np.zeros((16, seq_total), ml_dtypes.bfloat16)
     basis_table = np.concatenate([first, second, third, first, second, first, rim])
+    gap = np.zeros((LANES - 2 * BAND, seq_total), ml_dtypes.bfloat16)
     return (
         basis_table,
+        np.concatenate([first, second, gap]).T.copy(),
         *halves(fwd),
         *halves(back),
         *halves(inner),
@@ -130,6 +132,7 @@
     decay_ref,
     skip_ref,
     basis_hbm,
+    turned_hbm,
     fwd_hi_hbm,
     fwd_lo_hbm,
     back_hi_hbm,
@@ -139,11 +142,14 @@
     inv_hi_hbm,
     inv_lo_hbm,
     twiddle_hbm,
-    mq_out,
-    kv_out,
+    mixed_out,
+    query_out,
+    key_out,
+    value_out,
     proj_out,
     basis_out,
     basis_ref,
+    turned_ref,
     fwd_hi,
     fwd_lo,
     back_hi,
@@ -158,10 +164,17 @@
     turn_buf,
     wide_buf,
     raw_in,
-    mq_send,
-    kv_send,
-    mq_back,
-    kv_back,
+    long_send,
+    back_send,
+    long_back,
+    back_in,
+    rim_send,
+    rim_in,
+    end_send,
+    end_in,
+    query_buf,
+    key_buf,
+    value_buf,
     act_buf,
     cos_buf,
     filt_buf,
@@ -226,28 +239,12 @@
                 (inv_lo_hbm, inv_lo),
                 (back_hi_hbm, back_hi),
                 (back_lo_hbm, back_lo),
+                (turned_hbm, turned_ref),
             ]
         )
     ]
     for load in loads:
         load.start()
-
-    def pack(source, target, index):
-        wide = source[...].astype(F32)
-        for other in range(ctx_size):
-            target[other, index] = jnp.concatenate(
-                [
-                    wide[other * chans : (other + 1) * chans, fold * LANES : (fold + 1) * LANES]
-                    for fold in range(slab // chans)
-                ],
-                axis=0,
-            ).astype(BF16)
-
-    pack(key_ref, raw_ref, 0)
-    pack(value_ref, raw_ref, 1)
-    pack(query_ref, raw_ref, 2)
-    pack(grad_ref, raw_ref, 3)
-    pl.semaphore_wait(barrier, ctx_size + tp_size - 2)
 
     def push(src, dst, lane, ctx, tp):
         pltpu.make_async_remote_copy(
@@ -262,9 +259,6 @@
     def settle(ref, sem, count):
         part = ref.at[pl.ds(0, count)]
         pltpu.make_async_copy(part, part, sem).wait()
-
-    others(lambda peer: push(raw_ref.at[peer], raw_in.at[me], 0, peer, my_tp))
-    raw_in[me] = raw_ref[me]
 
     def expm1(value):
         series = 1.0 + value * (1.0 / 12.0)
@@ -287,11 +281,40 @@
     if chans < 8:
         params = jnp.concatenate([params] * (8 // chans), axis=0)
 
+    folds = slab // chans
+    tile_lanes = lax.broadcasted_iota(jnp.int32, (proj_ref.shape[1], LANES), 1)
+    next_ctx = jnp.where(me == ctx_size - 1, 0, me + 1)
+    prev_ctx = jnp.where(me == 0, ctx_size - 1, me - 1)
+
+    def tiles(ref):
+        wide = ref[...].astype(F32)
+        return [wide[:, fold * LANES : (fold + 1) * LANES] for fold in range(folds)]
+
+    def put(ref, parts):
+        for fold in range(folds):
+            ref[:, fold * LANES : (fold + 1) * LANES] = parts[fold].astype(ref.dtype)
+
+    def tap(which, offset):
+        at = feat + which * taps + offset
+        return jnp.broadcast_to(turn_buf[:, at : at + 1], tile_lanes.shape)
+
+    query, key, value = tiles(query_ref), tiles(key_ref), tiles(value_ref)
+    rim_send[...] = jnp.where(
+        tile_lanes >= LANES - 16,
+        query[-1],
+        jnp.where(
+            tile_lanes >= LANES - 32,
+            pltpu.roll(key[-1], LANES - 16, 1),
+            pltpu.roll(value[-1], LANES - 32, 1),
+        ),
+    ).astype(BF16)
+    pl.semaphore_wait(barrier, ctx_size + tp_size - 2)
+    push(rim_send, rim_in, 0, next_ctx, my_tp)
+
     def column(index):
         wide = jnp.broadcast_to(params[:, index : index + 1], (8, LANES))
         return jnp.concatenate([wide] * (rows // 8), axis=0)
 
-    tap_at = feat
     decay = column(after)
     inv_energy = column(after + 1)
     skip = column(after + 2)
@@ -329,15 +352,17 @@
         axis=0,
     ).astype(BF16)
 
-    def filter_step(index, carry):
-        start = pl.multiple_of(index * chunk, chunk)
-        here = pl.ds(start, chunk)
+    def activate(here):
         hidden = dot(w_stack, basis_ref[:, here])
         act, cosine = sine_cosine(hidden)
         cos_buf[:, here] = cosine
         act_hi, act_lo = split(act)
         act_buf[0:feat, here] = act_hi
         act_buf[feat : 2 * feat, here] = act_lo
+
+    def filter_step(index, carry):
+        here = pl.ds(pl.multiple_of(index * chunk, chunk), chunk)
+        activate(here)
         both = dot(proj_stack, act_buf[:, here])
         piece = both[0:8] + both[8:16]
         for block in range(chunk // LANES):
@@ -348,8 +373,53 @@
         return carry
 
     loads[0].wait()
-    lax.fori_loop(0, seq_total // chunk, filter_step, 0)
-    filt = (filt_buf[...] * envelope).astype(BF16)
+    steps = seq_total // chunk
+    if chans % 8 == 0:
+        for index in range(steps // 2):
+            activate(pl.ds(index * chunk, chunk))
+
+    pltpu.make_async_copy(rim_in, rim_in, recv_sems.at[0]).wait()
+    rim = jnp.where(me == 0, 0.0, rim_in[...].astype(F32))
+
+    def featurize(parts, before, which):
+        result = [tap(which, 0) * part for part in parts]
+        for offset in range(1, taps):
+            turned = [pltpu.roll(part, offset, 1) for part in [before, *parts]]
+            weight_here = tap(which, offset)
+            for fold in range(folds):
+                shifted = jnp.where(tile_lanes < offset, turned[fold], turned[fold + 1])
+                result[fold] = result[fold] + weight_here * shifted
+        return result
+
+    def pack(parts, index):
+        for other in range(ctx_size):
+            raw_ref[other, index] = jnp.concatenate(
+                [part[other * chans : (other + 1) * chans] for part in parts], axis=0
+            ).astype(BF16)
+
+    query_feat = featurize(query, rim, 0)
+    key_feat = featurize(key, pltpu.roll(rim, 16, 1), 1)
+    value_feat = featurize(value, pltpu.roll(rim, 32, 1), 2)
+    put(query_buf, query_feat)
+    put(key_buf, key_feat)
+    put(value_buf, value_feat)
+    pack([left * right for left, right in zip(key_feat, value_feat)], 0)
+    pack([left * right for left, right in zip(query_feat, tiles(grad_ref))], 1)
+    others(lambda peer: push(raw_ref.at[peer], raw_in.at[me], 3, peer, my_tp))
+    raw_in[me] = raw_ref[me]
+
+    if chans % 8 == 0:
+        for index in range(steps // 2, steps):
+            activate(pl.ds(index * chunk, chunk))
+        both = dot(proj_stack, act_buf[...])
+        piece = both[0:8] + both[8:16]
+        filt = jnp.concatenate(
+            [piece[:, block * LANES : (block + 1) * LANES] for block in range(blocks)], axis=0
+        )
+    else:
+        lax.fori_loop(0, steps, filter_step, 0)
+        filt = filt_buf[...]
+    filt = (filt * envelope).astype(BF16)
 
     blank = jnp.zeros((chans, LANES), F32)
 
@@ -399,62 +469,50 @@
             rows_buf[source * slab : (source + 1) * slab, :] = ref[source, index].astype(F32)
         return rows_buf[...]
 
-    def from_rows(ref, index, value):
+    def from_rows(ref, value):
         if slab % 16 == 0:
-            ref[:, index] = value.reshape(ctx_size, slab, LANES)
+            ref[...] = value.reshape(ctx_size, slab, LANES)
         else:
             rows_buf[...] = value.astype(F32)
             for target in range(ctx_size):
-                ref[target, index] = rows_buf[target * slab : (target + 1) * slab, :].astype(BF16)
-
-    def down(value):
-        if chans % 8 == 0:
-            return jnp.concatenate([blank, value[: rows - chans]], axis=0)
-        return jnp.where(row_ids < chans, 0.0, pltpu.roll(value, chans, 0))
-
-    def up(value):
-        if chans % 8 == 0:
-            return jnp.concatenate([value[chans:], blank], axis=0)
-        return jnp.where(row_ids >= rows - chans, 0.0, pltpu.roll(value, rows - chans, 0))
-
-    def featurize(signal, which):
-        result = column(tap_at + which * taps) * signal
+                ref[target] = rows_buf[target * slab : (target + 1) * slab, :].astype(BF16)
+
+    def to_tiles(ref):
+        pieces = [ref[source].astype(F32) for source in range(ctx_size)]
+        return [
+            jnp.concatenate(
+                [piece[fold * chans : (fold + 1) * chans] for piece in pieces], axis=0
+            )
+            for fold in range(folds)
+        ]
+
+    def featurize_back(parts, after_it, which):
+        result = [tap(which, 0) * part for part in parts]
         for offset in range(1, taps):
-            turned = pltpu.roll(signal, offset, 1)
-            shifted = jnp.where(lane_ids < offset, down(turned), turned)
-            result = result + column(tap_at + which * taps + offset) * shifted
-        return result
-
-    def featurize_back(signal, which):
-        result = column(tap_at + which * taps) * signal
-        for offset in range(1, taps):
-            turned = pltpu.roll(signal, LANES - offset, 1)
-            shifted = jnp.where(lane_ids >= LANES - offset, up(turned), turned)
-            result = result + column(tap_at + which * taps + offset) * shifted
+            turned = [pltpu.roll(part, LANES - offset, 1) for part in [*parts, after_it]]
+            weight_here = tap(which, offset)
+            for fold in range(folds):
+                shifted = jnp.where(
+                    tile_lanes >= LANES - offset, turned[fold + 1], turned[fold]
+                )
+                result[fold] = result[fold] + weight_here * shifted
         return result
 
     for load in loads[1:]:
         load.wait()
     ((filt_re, filt_im),) = spectra([filt])
 
-    settle(raw_in, recv_sems.at[0], ctx_size - 1)
-    key_feat = featurize(to_rows(raw_in, 0), 1)
-    value_feat = featurize(to_rows(raw_in, 1), 2)
-    query_feat = featurize(to_rows(raw_in, 2), 0)
-    grad_wide = to_rows(raw_in, 3)
-    carried = (key_feat * value_feat).astype(BF16)
-    grad_long = (grad_wide * query_feat).astype(BF16)
+    settle(raw_in, recv_sems.at[3], ctx_size - 1)
+    carried = to_rows(raw_in, 0).astype(BF16)
+    grad_long = to_rows(raw_in, 1).astype(BF16)
     (carried_re, carried_im), (grad_re, grad_im) = spectra([carried, grad_long])
 
     long_out = restore(
         filt_re * carried_re - filt_im * carried_im, filt_re * carried_im + filt_im * carried_re
     )
-    long_out = (long_out + skip * carried.astype(F32)).astype(BF16).astype(F32)
-
-    from_rows(mq_send, 0, (query_feat * long_out).astype(BF16))
-    grad_query_feat = (grad_wide * long_out).astype(BF16).astype(F32)
-    from_rows(mq_send, 1, featurize_back(grad_query_feat, 0).astype(BF16))
-    others(lambda peer: push(mq_send.at[peer], mq_back.at[me], 2, peer, my_tp))
+    from_rows(long_send, (long_out + skip * carried.astype(F32)).astype(BF16))
+    others(lambda peer: push(long_send.at[peer], long_back.at[me], 2, peer, my_tp))
+    long_back[me] = long_send[me]
 
     filter_grad = restore(
         carried_re * grad_re + carried_im * grad_im, carried_re * grad_im - carried_im * grad_re
@@ -483,7 +541,7 @@
     raw_hi = raw_hi.astype(F32)
     raw_lo = raw_lo.astype(F32)
     raw_two = jnp.concatenate([raw_hi, raw_lo], axis=0).astype(BF16)
-    gp_all = dot_lanes(raw_two, act_buf[...])
+    gp_all = jnp.transpose(dot_lanes(act_buf[...], raw_two))
     gp_all = gp_all[0:8] + gp_all[8:16]
     gp = gp_all + pltpu.roll(gp_all, feat, 1)
     gp = gp[0:chans] * (1.0 / math.sqrt(seq_total))
@@ -497,7 +555,7 @@
     grad_hidden = dot(pt_stack, raw_four) * cos_buf[...]
     gh_hi, gh_lo = split(grad_hidden)
     gh_stack = jnp.concatenate([gh_hi, gh_lo], axis=0)
-    gb_all = dot_lanes(gh_stack, basis_ref[0:LANES, :])
+    gb_all = dot(gh_stack, turned_ref[...])
     gb_all = gb_all[:feat] + gb_all[feat:]
     gb = (gb_all + pltpu.roll(gb_all, LANES - BAND, 1)) * math.sqrt(
         feat / (seq_total * tp_chans)
@@ -512,72 +570,61 @@
     carried_grad = restore(
         filt_re * grad_re + filt_im * grad_im, filt_re * grad_im - filt_im * grad_re
     )
-    carried_grad = (carried_grad + skip * grad_long.astype(F32)).astype(BF16).astype(F32)
-    grad_key_feat = (carried_grad * value_feat).astype(BF16).astype(F32)
-    grad_value_feat = (carried_grad * key_feat).astype(BF16).astype(F32)
-    from_rows(kv_send, 0, featurize_back(grad_key_feat, 1).astype(BF16))
-    from_rows(kv_send, 1, featurize_back(grad_value_feat, 2).astype(BF16))
+    from_rows(back_send, (carried_grad + skip * grad_long.astype(F32)).astype(BF16))
+    others(lambda peer: push(back_send.at[peer], back_in.at[me], 6, peer, my_tp))
+    back_in[me] = back_send[me]
     settle(part_in, recv_sems.at[1], ctx_size - 1)
     half_buf[my_tp] = jnp.sum(part_in[:, chans : chans + share], axis=0)
     tp_others(lambda peer: push(half_buf.at[my_tp], half_buf.at[my_tp], 4, me, peer))
-    others(lambda peer: push(kv_send.at[peer], kv_back.at[me], 3, peer, my_tp))
+
+    settle(long_back, recv_sems.at[2], ctx_size - 1)
+    long_tok = to_tiles(long_back)
+    put(mixed_out, [left * right for left, right in zip(tiles(query_buf), long_tok)])
+
+    def rounded(left, right):
+        return [(one * two).astype(BF16).astype(F32) for one, two in zip(left, right)]
+
+    grad_query_feat = rounded(tiles(grad_ref), long_tok)
 
     settle(half_buf, recv_sems.at[4], tp_size - 1)
     sum_buf[...] = jnp.sum(half_buf[...], axis=0)
     others(lambda peer: push(sum_buf, sum_in.at[me], 5, peer, my_tp))
     sum_in[me] = sum_buf[...]
-    mq_back[me] = mq_send[me]
-    kv_back[me] = kv_send[me]
-    proj_out[...] = part_in[:, 0:chans]
-    settle(mq_back, recv_sems.at[2], ctx_size - 1)
-    mq_out[...] = mq_back[...]
-    settle(kv_back, recv_sems.at[3], ctx_size - 1)
-    kv_out[...] = kv_back[...]
+
+    settle(back_in, recv_sems.at[6], ctx_size - 1)
+    carried_tok = to_tiles(back_in)
+    grad_key_feat = rounded(carried_tok, tiles(value_buf))
+    grad_value_feat = rounded(carried_tok, tiles(key_buf))
+    end_send[...] = jnp.where(
+        tile_lanes < 16,
+        grad_query_feat[0],
+        jnp.where(
+            tile_lanes < 32,
+            pltpu.roll(grad_key_feat[0], 16, 1),
+            pltpu.roll(grad_value_feat[0], 32, 1),
+        ),
+    ).astype(BF16)
+    push(end_send, end_in, 7, prev_ctx, my_tp)
+    proj = jnp.concatenate([part_in[source, 0:chans] for source in range(ctx_size)], axis=0)
+    proj_out[...] = jnp.transpose(proj)[:feat]
     settle(sum_in, recv_sems.at[5], ctx_size - 1)
-    basis_out[...] = sum_in[...]
-
-    settle(raw_in, send_sems.at[0], ctx_size - 1)
+    basis = jnp.concatenate([sum_in[source] for source in range(ctx_size)], axis=0)
+    basis_out[...] = jnp.transpose(basis)[:emb]
+
+    pltpu.make_async_copy(end_in, end_in, recv_sems.at[7]).wait()
+    end = jnp.where(me == ctx_size - 1, 0.0, end_in[...].astype(F32))
+    put(query_out, featurize_back(grad_query_feat, end, 0))
+    put(key_out, featurize_back(grad_key_feat, pltpu.roll(end, LANES - 16, 1), 1))
+    put(value_out, featurize_back(grad_value_feat, pltpu.roll(end, LANES - 32, 1), 2))
+
+    pltpu.make_async_copy(rim_in, rim_in, send_sems.at[0]).wait()
     settle(part_in, send_sems.at[1], ctx_size - 1)
-    settle(mq_back, send_sems.at[2], ctx_size - 1)
-    settle(kv_back, send_sems.at[3], ctx_size - 1)
+    settle(long_back, send_sems.at[2], ctx_size - 1)
+    settle(raw_in, send_sems.at[3], ctx_size - 1)
     settle(half_buf, send_sems.at[4], tp_size - 1)
     settle(sum_in, send_sems.at[5], ctx_size - 1)
-
-
-def unpack_kernel(
-    dims,
-    mq_ref,
-    kv_ref,
-    proj_ref,
-    basis_ref,
-    mixed_out,
-    query_out,
-    key_out,
-    value_out,
-    proj_out,
-    basis_out,
-):
-    ctx_size, chans, folds, share = dims
-    feat = ctx_size * share
-    group = max(1, 16 // chans)
-    for source, index, target in (
-        (mq_ref, 0, mixed_out),
-        (mq_ref, 1, query_out),
-        (kv_ref, 0, key_out),
-        (kv_ref, 1, value_out),
-    ):
-        for first in range(0, ctx_size, group):
-            pieces = [source[first + other, index].astype(F32) for other in range(group)]
-            for fold in range(folds):
-                target[
-                    first * chans : (first + group) * chans, fold * LANES : (fold + 1) * LANES
-                ] = jnp.concatenate(
-                    [piece[fold * chans : (fold + 1) * chans] for piece in pieces], axis=0
-                ).astype(BF16)
-    proj = jnp.concatenate([proj_ref[source] for source in range(ctx_size)], axis=0)
-    proj_out[...] = jnp.transpose(proj)[:feat]
-    basis = jnp.concatenate([basis_ref[source] for source in range(ctx_size)], axis=0)
-    basis_out[...] = jnp.transpose(basis)[: basis_out.shape[0]]
+    settle(back_in, send_sems.at[6], ctx_size - 1)
+    pltpu.make_async_copy(end_in, end_in, send_sems.at[7]).wait()
 
 
 def on_device(
@@ -606,21 +653,24 @@
     rows = blocks * chans
 
     share = feat // ctx_size
-    raw_slabs = (ctx_size, 4, slab, LANES)
-    slabs = (ctx_size, 2, slab, LANES)
+    raw_slabs = (ctx_size, 2, slab, LANES)
+    slabs = (ctx_size, slab, LANES)
     dims = (ctx_size, tp_size, chans, seq_total, taps, feat, emb, chan_local * tp_size)
     vmem = pl.BlockSpec(memory_space=pltpu.VMEM)
     anywhere = pl.BlockSpec(memory_space=pl.ANY)
-    landed = pl.pallas_call(
+    block = jax.ShapeDtypeStruct((chan_local, num_tok), BF16)
+    mixed, grad_query, grad_key, grad_value, proj_turned, basis_turned = pl.pallas_call(
         functools.partial(mixer_kernel, dims),
         out_shape=(
-            jax.ShapeDtypeStruct(slabs, BF16),
-            jax.ShapeDtypeStruct(slabs, BF16),
-            jax.ShapeDtypeStruct((ctx_size, chans, LANES), F32),
-            jax.ShapeDtypeStruct((ctx_size, share, LANES), F32),
+            block,
+            block,
+            block,
+            block,
+            jax.ShapeDtypeStruct((feat, chan_local), F32),
+            jax.ShapeDtypeStruct((emb, feat), F32),
         ),
         in_specs=[vmem] * 10 + [anywhere] * len(tables),
-        out_specs=(vmem, vmem, vmem, vmem),
+        out_specs=(vmem,) * 6,
         scratch_shapes=[pltpu.VMEM(table.shape, table.dtype) for table in tables]
         + [
             pltpu.VMEM(raw_slabs, BF16),
@@ -632,6 +682,13 @@
             pltpu.VMEM(slabs, BF16),
             pltpu.VMEM(slabs, BF16),
             pltpu.VMEM(slabs, BF16),
+            pltpu.VMEM((chan_local, LANES), BF16),
+            pltpu.VMEM((chan_local, LANES), BF16),
+            pltpu.VMEM((chan_local, LANES), BF16),
+            pltpu.VMEM((chan_local, LANES), BF16),
+            pltpu.VMEM((chan_local, num_tok), F32),
+            pltpu.VMEM((chan_local, num_tok), F32),
+            pltpu.VMEM((chan_local, num_tok), F32),
             pltpu.VMEM((2 * feat, seq_total), BF16),
             pltpu.VMEM((feat, seq_total), F32),
             pltpu.VMEM((rows, LANES), F32),
@@ -641,8 +698,8 @@
             pltpu.VMEM((tp_size, share, LANES), F32),
             pltpu.VMEM((share, LANES), F32),
             pltpu.VMEM((ctx_size, share, LANES), F32),
-            pltpu.SemaphoreType.DMA((6,)),
-            pltpu.SemaphoreType.DMA((6,)),
+            pltpu.SemaphoreType.DMA((8,)),
+            pltpu.SemaphoreType.DMA((8,)),
             pltpu.SemaphoreType.DMA((len(tables),)),
         ],
         compiler_params=pltpu.CompilerParams(
@@ -661,20 +718,6 @@
         skip_gain[None, :],
         *tables,
     )
-    block = jax.ShapeDtypeStruct((chan_local, num_tok), BF16)
-    mixed, grad_query, grad_key, grad_value, proj_turned, basis_turned = pl.pallas_call(
-        functools.partial(unpack_kernel, (ctx_size, chans, folds, share)),
-        out_shape=(
-            block,
-            block,
-            block,
-            block,
-            jax.ShapeDtypeStruct((feat, chan_local), F32),
-            jax.ShapeDtypeStruct((emb, feat), F32),
-        ),
-        in_specs=[vmem] * 4,
-        out_specs=(vmem,) * 6,
-    )(*landed)
     return (mixed, grad_query, grad_key, grad_value, proj_turned.T, basis_turned.T)
 
 

time: 33.6 us -> 41.2 us (1.23)
  local copies, waits for them, and re-layouts: 0 us -> 8.6 us
  Pallas kernels: 32.7 us -> 31.5 us
    unnamed x0 -> x6, local copies, waits for them, and re-layouts: none -> 8.6 us
    pallas_call x2 -> x1, Pallas kernels: 32.7 us -> 31.5 us  [on_device(): pl.pallas_call(functools.partial(mixer_kernel, dims), out_shape=(block, b...]
where the time goes in v5:
time: 41.2 us; the launch traced here: 40.7 us
  Pallas kernels  31.5 us (76%)
  local copies, waits for them, and re-layouts  8.6 us (21%)
  between operations  0.65 us (2%)
    pallas_call x1, Pallas kernels, on_device(): pl.pallas_call(functools.partial(mixer_kernel, dims), out_shape=(block, b...  31.5 us
    unnamed x6, local copies, waits for them, and re-layouts  8.6 us

profile of v5, /device:TPU:0, one launch (start us, length us, event | category | flops | bytes accessed | tf_op | source)
XLA Modules:
  0.0 40.7 jit_solution(805302891615526734)
XLA Ops:
  0.6 31.5 %shard_map.244 = (bf16[128,256]{1,0:T(8,128)(2,1)}, bf16[128,256]{1,0:T(8,128)(2,1)}, bf16[128,256]{1,0:T(8,128)(2,1)}, bf16[128,256]{1,0:T(8,128)(2,1)}, f32[64,128]{1,0:T(8,128)}, /*index=5*/f32[33,64]{1,0:T(8,128)}) custom-call(bf16[128,256]{1,0:T(8,128)(2,1)} %query_ref.1, bf16[128,256]{1,0:T(8,128)(2,1)} %key_ref.1, bf16[128,256]{1,0:T(8,128)(2,1)} %value_ref.1, ...), custom_call_target="tpu_custom_call" | custom-call | tf_op jit(solution)/shard_map/pallas_call | solution.py:662
  32.1 1.5 %copy.33 = bf16[128,256]{1,0:T(8,128)(2,1)} copy(bf16[128,256]{1,0:T(8,128)(2,1)} %get-tuple-element.24) | data formatting | bytes 131072
  33.6 1.5 %copy.34 = bf16[128,256]{1,0:T(8,128)(2,1)} copy(bf16[128,256]{1,0:T(8,128)(2,1)} %get-tuple-element.25) | data formatting | bytes 131072
  35.1 1.5 %copy.35 = bf16[128,256]{1,0:T(8,128)(2,1)} copy(bf16[128,256]{1,0:T(8,128)(2,1)} %get-tuple-element.26) | data formatting | bytes 131072
  36.5 1.5 %copy.36 = bf16[128,256]{1,0:T(8,128)(2,1)} copy(bf16[128,256]{1,0:T(8,128)(2,1)} %get-tuple-element.27) | data formatting | bytes 131072
  38.0 1.4 %copy.37 = f32[128,64]{0,1:T(8,128)} copy(f32[128,64]{0,1:T(8,128)} %bitcast.9) | data formatting | bytes 65536
  39.4 1.3 %copy.38 = f32[64,33]{0,1:T(8,128)} copy(f32[64,33]{0,1:T(8,128)} %bitcast.11) | data formatting | bytes 16896

commit v6 on v4

--- a/solution.py
+++ b/solution.py
@@ -188,7 +188,7 @@
             body(jnp.where(other >= axis_size, other - axis_size, other))
             return carry
 
-        if axis_size <= 16:
+        if axis_size <= 2:
             for offset in range(1, axis_size):
                 step(offset, 0)
         else:
@@ -347,8 +347,12 @@
 
     loads[0].wait()
     if chans % 8 == 0:
-        for index in range(seq_total // chunk):
-            activate(pl.ds(index * chunk, chunk))
+
+        def activate_step(index, carry):
+            activate(pl.ds(pl.multiple_of(index * chunk, chunk), chunk))
+            return carry
+
+        lax.fori_loop(0, seq_total // chunk, activate_step, 0)
         both = dot(proj_stack, act_buf[...])
         piece = both[0:8] + both[8:16]
         filt = jnp.concatenate(
@@ -525,10 +529,10 @@
     grad_value_feat = (carried_grad * key_feat).astype(BF16).astype(F32)
     from_rows(kv_send, 0, featurize_back(grad_key_feat, 1).astype(BF16))
     from_rows(kv_send, 1, featurize_back(grad_value_feat, 2).astype(BF16))
+    others(lambda peer: push(kv_send.at[peer], kv_back.at[me], 3, peer, my_tp))
     settle(part_in, recv_sems.at[1], ctx_size - 1)
     half_buf[my_tp] = jnp.sum(part_in[:, chans : chans + share], axis=0)
     tp_others(lambda peer: push(half_buf.at[my_tp], half_buf.at[my_tp], 4, me, peer))
-    others(lambda peer: push(kv_send.at[peer], kv_back.at[me], 3, peer, my_tp))
 
     settle(half_buf, recv_sems.at[4], tp_size - 1)
     sum_buf[...] = jnp.sum(half_buf[...], axis=0)

time: 33.3 us -> 35 us (1.051)
  Pallas kernels: 32.5 us -> 34.2 us
    pallas_call x1, Pallas kernels: 30.8 us -> 32.5 us  [on_device(): pl.pallas_call(functools.partial(mixer_kernel, dims), out_shape=(jax.Shap...]
where the time goes in v6:
time: 35 us; the launch traced here: 34.8 us
  Pallas kernels  34.2 us (98%)
  between operations  0.64 us (2%)
    pallas_call x1, Pallas kernels, on_device(): pl.pallas_call(functools.partial(mixer_kernel, dims), out_shape=(jax.Shap...  32.5 us
    pallas_call x1, Pallas kernels, on_device(): pl.pallas_call(functools.partial(unpack_kernel, (ctx_size, chans, folds,...  1.7 us

profile of v6, /device:TPU:0, one launch (start us, length us, event | category | flops | bytes accessed | tf_op | source)
XLA Modules:
  0.0 34.8 jit_solution(10320929291014730463)
XLA Ops:
  0.6 32.5 %shard_map.217 = (bf16[16,2,16,128]{3,2,1,0:T(8,128)(2,1)}, bf16[16,2,16,128]{3,2,1,0:T(8,128)(2,1)}, f32[16,8,128]{2,1,0:T(8,128)}, f32[16,4,128]{2,1,0:T(4,128)}) custom-call(bf16[128,256]{1,0:T(8,128)(2,1)} %query_ref.1, bf16[128,256]{1,0:T(8,128)(2,1)} %key_ref.1, bf16[128,256]{1,0:T(8,128)(2,1)} %value_ref.1, bf16[128,256]{1,0:T(8,128)(2,1)} %grad_ref.1, ...), custom_call_target="tpu_custom_call" | custom-call | tf_op jit(solution)/shard_map/pallas_call | solution.py:626
  33.1 1.7 %shard_map.218 = (bf16[128,256]{1,0:T(8,128)(2,1)}, bf16[128,256]{1,0:T(8,128)(2,1)}, bf16[128,256]{1,0:T(8,128)(2,1)}, bf16[128,256]{1,0:T(8,128)(2,1)}, f32[64,128]{1,0:T(8,128)}, /*index=5*/f32[33,64]{1,0:T(8,128)}) custom-call(bf16[16,2,16,128]{3,2,1,0:T(8,128)(2,1)} %get-tuple-element.16.mq_ref, bf16[16,2,16,128]{3,2,1,0:T(8,128)(2,1)} %get-tuple-element.17.kv_ref, ...), custom_call_target="tpu_custom_call" | custom-call | tf_op jit(solution)/shard_map/pallas_call | solution.py:677
